TPU v7x, 512 devices: a whole 4x8x8 slice. The times are simulated.
512 devices in a mesh: blk: 32 (over z_lo, y, core), space: 16 (over x, z_hi).
Axes of the slice: x: 4, y: 8, z: 8 (z_hi: 4, z_lo: 2; z = z_hi * 2 + z_lo), core: 2. Of those that a mesh axis runs over, the one named last changes fastest.
Arguments:
- input_field: bfloat16 [128, 96, 96, 192], P('blk', 'space'), may hold values from -6 to 6
- cotangent: bfloat16 [128, 96, 96, 192], P('blk', 'space'), may hold values from -0.59765625 to 0.59765625
- weights: bfloat16 [16, 32, 8, 2, 128, 128], P('space', 'blk'), may hold values from -0.375 to 0.375
Outputs:
- spectral_out: bfloat16 [128, 96, 96, 192], P('blk', 'space')
- field_grad: bfloat16 [128, 96, 96, 192], P('blk', 'space')
- weight_grad: float32 [16, 32, 8, 2, 128, 128], P('space', 'blk')
All inputs are finite; a program needn't handle non-finite values.
Results may differ from a plain program's by a relative error of at most 0.015.
Values may be sent and summed in bfloat16 or wider, within the bound.
No kernel may reach another device: no remote copies, remote signals or barrier semaphores. Data moves between devices by JAX's collectives and lax.ppermute only.
A program may use at most 64 MiB of HBM per device.

v0:
```python
import math

import jax
import jax.numpy as jnp
from jax import lax
from jax.sharding import PartitionSpec as P

NX = 96
NY = 192
NZ = 96
MX = 16
MY = 32
MZ = 8


def centered_freqs(total_count):
    indices = jnp.arange(total_count, dtype=jnp.int32)
    return jnp.where(indices < total_count // 2, indices, indices - total_count)


def phase_pair(frequencies, positions, length):
    product = frequencies[:, None] * positions[None, :] % length
    angles = product.astype(jnp.float32) * (2.0 * math.pi / length)
    return (jnp.cos(angles), jnp.sin(angles))


def x_analysis_table():
    cosines, sine_values = phase_pair(centered_freqs(MX), jnp.arange(NX, dtype=jnp.int32), NX)
    return jnp.stack([cosines.T, -sine_values.T], 1).astype(jnp.bfloat16)


def y_analysis_table():
    cosines, sine_values = phase_pair(centered_freqs(MY), jnp.arange(NY, dtype=jnp.int32), NY)
    real_rows = jnp.stack([cosines.T, -sine_values.T], 1)
    imag_rows = jnp.stack([sine_values.T, cosines.T], 1)
    return jnp.stack([real_rows, imag_rows], 0).astype(jnp.bfloat16)


def z_analysis_table(positions):
    cosines, sine_values = phase_pair(jnp.arange(MZ, dtype=jnp.int32), positions, NZ)
    real_rows = jnp.stack([cosines.T, -sine_values.T], 1)
    imag_rows = jnp.stack([sine_values.T, cosines.T], 1)
    return jnp.stack([real_rows, imag_rows], 0).astype(jnp.bfloat16)


def mode_weights():
    return jnp.where(jnp.arange(MZ) == 0, 1.0, 2.0).astype(jnp.float32)


def z_synthesis_table(positions, amplitude):
    cosines, sine_values = phase_pair(jnp.arange(MZ, dtype=jnp.int32), positions, NZ)
    cosines = cosines * amplitude[:, None]
    sine_values = sine_values * amplitude[:, None]
    real_rows = jnp.stack([cosines, sine_values], -1)
    imag_rows = jnp.stack([-sine_values, cosines], -1)
    return jnp.stack([real_rows, imag_rows], 1).astype(jnp.bfloat16)


def y_synthesis_table():
    cosines, sine_values = phase_pair(centered_freqs(MY), jnp.arange(NY, dtype=jnp.int32), NY)
    real_rows = jnp.stack([cosines, sine_values], 1)
    imag_rows = jnp.stack([-sine_values, cosines], 1)
    return jnp.stack([real_rows, imag_rows], 0).astype(jnp.bfloat16)


def x_synthesis_table():
    cosines, sine_values = phase_pair(centered_freqs(MX), jnp.arange(NX, dtype=jnp.int32), NX)
    return jnp.stack([cosines, -sine_values], 0).astype(jnp.bfloat16)


def contract(pattern, first_operand, second_operand):
    return jnp.einsum(pattern, first_operand, second_operand, preferred_element_type=jnp.float32)


def analyse(values, x_table, y_table):
    xsum = contract("czxy,xrp->czrpy", values, x_table).astype(jnp.bfloat16)
    return contract("czrpy,ryoq->czopq", xsum, y_table).astype(jnp.bfloat16)


def synthesize(zback, y_table, x_table):
    yback = contract("czipq,iqoy->czopy", zback, y_table).astype(jnp.bfloat16)
    return contract("czipy,ipx->czxy", yback, x_table).astype(jnp.bfloat16)


def scale_spectra(zsum_f, zsum_g, amplitude, forward_scale, synth_scale):
    spec_f = (zsum_f * forward_scale).astype(jnp.bfloat16)
    spec_g = (zsum_g * (amplitude * synth_scale)[None, :, None, None, None]).astype(jnp.bfloat16)
    return (spec_f, spec_g)


def shards(input_field, cotangent, weights):
    forward_scale = 1.0 / math.sqrt(NX * NY * NZ)
    synth_scale = 1.0 / math.sqrt(MX * MY * MZ)
    amplitude = mode_weights()
    unit_weights = jnp.ones((MZ,), jnp.float32)
    space_count = lax.axis_size("space")
    space_index = lax.axis_index("space")
    px_local = MX // space_count
    x_table = x_analysis_table()
    y_table = y_analysis_table()
    plane_f = analyse(input_field, x_table, y_table)
    plane_g = analyse(cotangent, x_table, y_table)
    pieces = (
        lax.all_gather(plane_f, "space", axis=1, tiled=True),
        lax.all_gather(plane_g, "space", axis=1, tiled=True),
    )
    row_count = pieces[0].shape[1]
    z_table = z_analysis_table(jnp.arange(row_count, dtype=jnp.int32))
    own_f = lax.dynamic_slice_in_dim(pieces[0], space_index * px_local, px_local, 3)
    own_g = lax.dynamic_slice_in_dim(pieces[1], space_index * px_local, px_local, 3)
    zsum_f = contract("czipq,izok->ckopq", own_f, z_table)
    zsum_g = contract("czipq,izok->ckopq", own_g, z_table)
    spec_f, spec_g = scale_spectra(zsum_f, zsum_g, amplitude, forward_scale, synth_scale)
    modes_f, modes_g = (
        lax.all_to_all(spec_f, "blk", split_axis=4, concat_axis=0, tiled=True),
        lax.all_to_all(spec_g, "blk", split_axis=4, concat_axis=0, tiled=True),
    )
    w_real = weights[:, :, :, 0]
    w_imag = weights[:, :, :, 1]
    f_real = modes_f[:, :, 0]
    f_imag = modes_f[:, :, 1]
    g_real = modes_g[:, :, 0]
    g_imag = modes_g[:, :, 1]
    mixed_real = contract("abkoc,ckab->okab", w_real, f_real) - contract(
        "abkoc,ckab->okab", w_imag, f_imag
    )
    mixed_imag = contract("abkoc,ckab->okab", w_real, f_imag) + contract(
        "abkoc,ckab->okab", w_imag, f_real
    )
    mixed = jnp.stack([mixed_real, mixed_imag], 2).astype(jnp.bfloat16)
    grad_real = contract("abkoc,okab->ckab", w_real, g_real) + contract(
        "abkoc,okab->ckab", w_imag, g_imag
    )
    grad_imag = contract("abkoc,okab->ckab", w_real, g_imag) - contract(
        "abkoc,okab->ckab", w_imag, g_real
    )
    grad_spec = jnp.stack([grad_real, grad_imag], 2).astype(jnp.bfloat16)
    wgrad_real = contract("okab,ckab->abkoc", g_real, f_real) + contract(
        "okab,ckab->abkoc", g_imag, f_imag
    )
    wgrad_imag = contract("okab,ckab->abkoc", g_imag, f_real) - contract(
        "okab,ckab->abkoc", g_real, f_imag
    )
    weight_grad = jnp.stack([wgrad_real, wgrad_imag], 3)
    all_positions = jnp.arange(NZ, dtype=jnp.int32)
    back_y, back_u = (
        lax.all_to_all(mixed, "blk", split_axis=0, concat_axis=4, tiled=True),
        lax.all_to_all(grad_spec, "blk", split_axis=0, concat_axis=4, tiled=True),
    )
    spread_y = (
        contract("ckipq,kizo->czopq", back_y, z_synthesis_table(all_positions, amplitude))
        * synth_scale
    ).astype(jnp.bfloat16)
    spread_u = (
        contract("ckipq,kizo->czopq", back_u, z_synthesis_table(all_positions, unit_weights))
        * forward_scale
    ).astype(jnp.bfloat16)
    zback_y, zback_u = (
        lax.all_to_all(spread_y, "space", split_axis=1, concat_axis=3, tiled=True),
        lax.all_to_all(spread_u, "space", split_axis=1, concat_axis=3, tiled=True),
    )
    y_back_table = y_synthesis_table()
    x_back_table = x_synthesis_table()
    spectral_out = synthesize(zback_y, y_back_table, x_back_table)
    field_grad = synthesize(zback_u, y_back_table, x_back_table)
    return (spectral_out, field_grad, weight_grad)


def solution(mesh):
    placed = (
        P("blk", "space", None, None),
        P("blk", "space", None, None),
        P("space", "blk", None, None, None, None),
    )
    return jax.shard_map(
        shards,
        mesh=mesh,
        in_specs=placed,
        out_specs=(
            P("blk", "space", None, None),
            P("blk", "space", None, None),
            P("space", "blk", None, None, None, None),
        ),
        check_vma=False,
    )
```

profile of v0, /device:TPU:1, one launch (start us, length us, event | category | flops | bytes accessed | tf_op | source)
XLA Modules:
  0.0 298.0 jit_solution(3452753942734966532)
XLA Ops:
  1.2 0.7 copy-done
  1.9 0.4 fusion.13
  2.4 113.0 %all_gather.6 = bf16[4,96,2,16,32]{4,3,1,0,2:T(8,128)(2,1)} all-gather(bf16[4,6,2,16,32]{4,3,1,0,2:T(8,128)(2,1)S(1)} %fusion.13), channel_id=1, replica_groups=mesh['blk'=32,'space'=16] {'space'}, dimensions={1}, use_global_device_ids=true | all-gather | bytes 835584 | tf_op jit(solution)/shard_map/all_gather | solution.py:104
  115.4 0.4 fusion.12
  115.8 79.5 %all_gather.7 = bf16[4,96,2,16,32]{4,3,1,0,2:T(8,128)(2,1)} all-gather(bf16[4,6,2,16,32]{4,3,1,0,2:T(8,128)(2,1)S(1)} %fusion.12), channel_id=1, replica_groups=mesh['blk'=32,'space'=16] {'space'}, dimensions={1}, use_global_device_ids=true | all-gather | bytes 835584 | tf_op jit(solution)/shard_map/all_gather | solution.py:105
  195.3 2.8 constant_dynamic-slice_fusion
  198.1 0.3 copy.41
  198.5 0.8 copy.42
  199.3 12.8 %all-to-all-start.3 = ((bf16[4,8,2,1,32]{1,0,2,3,4:T(4,128)(2,1)}), bf16[4,8,2,1,32]{1,0,2,3,4:T(4,128)(2,1)S(1)}, u32[]{:S(2)}, u32[]{:S(2)}) async-start(bf16[4,8,2,1,32]{1,0,2,3,4:T(4,128)(2,1)} %copy.42), calls=%async_computation.3 | async-start | bytes 131072 | tf_op jit(solution)/shard_map/all_to_all | solution.py:116
  212.6 0.3 copy.32
  213.2 0.7 copy.33
  213.9 6.3 %all-to-all-done.3 = bf16[4,8,2,1,32]{1,0,2,3,4:T(4,128)(2,1)S(1)} async-done(((bf16[4,8,2,1,32]{1,0,2,3,4:T(4,128)(2,1)}), bf16[4,8,2,1,32]{1,0,2,3,4:T(4,128)(2,1)S(1)}, u32[]{:S(2)}, u32[]{:S(2)}) %all-to-all-start.3) | async-done | bytes 4128 | tf_op jit(solution)/shard_map/all_to_all | solution.py:116
  220.2 4.8 %all-to-all-start = ((bf16[4,8,2,1,32]{1,0,2,3,4:T(4,128)(2,1)}), bf16[4,8,2,1,32]{1,0,2,3,4:T(4,128)(2,1)S(1)}, u32[]{:S(2)}, u32[]{:S(2)}) async-start(bf16[4,8,2,1,32]{1,0,2,3,4:T(4,128)(2,1)} %copy.33), calls=%async_computation | async-start | bytes 131072 | tf_op jit(solution)/shard_map/all_to_all | solution.py:115
  225.9 7.2 %all-to-all-done = bf16[4,8,2,1,32]{1,0,2,3,4:T(4,128)(2,1)S(1)} async-done(((bf16[4,8,2,1,32]{1,0,2,3,4:T(4,128)(2,1)}), bf16[4,8,2,1,32]{1,0,2,3,4:T(4,128)(2,1)S(1)}, u32[]{:S(2)}, u32[]{:S(2)}) %all-to-all-start) | async-done | bytes 4128 | tf_op jit(solution)/shard_map/all_to_all | solution.py:115
  233.2 0.3 fusion.36
  233.8 0.3 fusion.44
  234.6 0.8 copy.44
  235.4 4.8 %all-to-all-start.4 = ((bf16[128,8,2,1,1]{1,2,4,3,0:T(2,128)(2,1)}), bf16[128,8,2,1,1]{1,2,4,3,0:T(2,128)(2,1)S(1)}, u32[]{:S(2)}, u32[]{:S(2)}) async-start(bf16[128,8,2,1,1]{1,2,4,3,0:T(2,128)(2,1)} %copy.44), calls=%async_computation.4 | async-start | bytes 131072 | tf_op jit(solution)/shard_map/all_to_all | solution.py:148
  240.1 0.3 add_bitcast_fusion
  240.5 1.1 pad_maximum_fusion
  241.6 0.8 copy.35
  242.3 6.0 %all-to-all-done.4 = bf16[128,8,2,1,1]{1,2,4,3,0:T(2,128)(2,1)S(1)} async-done(((bf16[128,8,2,1,1]{1,2,4,3,0:T(2,128)(2,1)}), bf16[128,8,2,1,1]{1,2,4,3,0:T(2,128)(2,1)S(1)}, u32[]{:S(2)}, u32[]{:S(2)}) %all-to-all-start.4) | async-done | bytes 4128 | tf_op jit(solution)/shard_map/all_to_all | solution.py:148
  248.3 4.8 %all-to-all-start.1 = ((bf16[128,8,2,1,1]{1,2,4,3,0:T(2,128)(2,1)}), bf16[128,8,2,1,1]{1,2,4,3,0:T(2,128)(2,1)S(1)}, u32[]{:S(2)}, u32[]{:S(2)}) async-start(bf16[128,8,2,1,1]{1,2,4,3,0:T(2,128)(2,1)} %copy.35), calls=%async_computation.1 | async-start | bytes 131072 | tf_op jit(solution)/shard_map/all_to_all | solution.py:147
  253.6 0.8 reshape.864
  254.4 6.9 %all-to-all-done.1 = bf16[128,8,2,1,1]{1,2,4,3,0:T(2,128)(2,1)S(1)} async-done(((bf16[128,8,2,1,1]{1,2,4,3,0:T(2,128)(2,1)}), bf16[128,8,2,1,1]{1,2,4,3,0:T(2,128)(2,1)S(1)}, u32[]{:S(2)}, u32[]{:S(2)}) %all-to-all-start.1) | async-done | bytes 4128 | tf_op jit(solution)/shard_map/all_to_all | solution.py:147
  261.2 13.5 %all-to-all-start.5 = ((bf16[16,2,768]{2,1,0:T(2,128)(2,1)}), bf16[16,2,768]{2,1,0:T(2,128)(2,1)S(1)}, u32[]{:S(2)}, u32[]{:S(2)}) async-start(bf16[16,2,768]{2,1,0:T(2,128)(2,1)} %reshape.864), calls=%async_computation.5 | async-start | bytes 98304 | tf_op jit(solution)/shard_map/all_to_all | solution.py:160
  275.2 0.8 reshape.862
  276.0 7.7 %all-to-all-done.5 = bf16[16,2,768]{2,1,0:T(2,128)(2,1)S(1)} async-done(((bf16[16,2,768]{2,1,0:T(2,128)(2,1)}), bf16[16,2,768]{2,1,0:T(2,128)(2,1)S(1)}, u32[]{:S(2)}, u32[]{:S(2)}) %all-to-all-start.5) | async-done | bytes 49184 | tf_op jit(solution)/shard_map/all_to_all | solution.py:160
  283.8 3.5 %all-to-all-start.2 = ((bf16[16,2,768]{2,1,0:T(2,128)(2,1)}), bf16[16,2,768]{2,1,0:T(2,128)(2,1)S(1)}, u32[]{:S(2)}, u32[]{:S(2)}) async-start(bf16[16,2,768]{2,1,0:T(2,128)(2,1)} %reshape.862), calls=%async_computation.2 | async-start | bytes 98304 | tf_op jit(solution)/shard_map/all_to_all | solution.py:159
  287.4 1.7 fusion.1
  289.1 7.1 %all-to-all-done.2 = bf16[16,2,768]{2,1,0:T(2,128)(2,1)S(1)} async-done(((bf16[16,2,768]{2,1,0:T(2,128)(2,1)}), bf16[16,2,768]{2,1,0:T(2,128)(2,1)S(1)}, u32[]{:S(2)}, u32[]{:S(2)}) %all-to-all-start.2) | async-done | bytes 49184 | tf_op jit(solution)/shard_map/all_to_all | solution.py:159
  296.4 1.7 fusion
  (57 shorter events, 4.5 us)
Async XLA Ops:
  0.6 1.3 copy-start
  2.4 113.0 %copy-start.2 = (bf16[4,6,96,192]{3,2,1,0:T(8,128)(2,1)S(1)}, bf16[4,6,96,192]{3,2,1,0:T(8,128)(2,1)}, u32[]{:S(2)}) copy-start(bf16[4,6,96,192]{3,2,1,0:T(8,128)(2,1)} %param.4) | copy-start | bytes 2654212
  198.1 27.0 %copy-start.1 = (bf16[1,1,8,2,128,128]{5,4,3,2,1,0:T(8,128)(2,1)S(1)}, bf16[1,1,8,2,128,128]{5,4,3,2,1,0:T(8,128)(2,1)}, u32[]{:S(2)}) copy-start(bf16[1,1,8,2,128,128]{5,4,3,2,1,0:T(8,128)(2,1)} %param.5) | copy-start | bytes 1572868
  199.3 20.8 %all-to-all-start.3 = ((bf16[4,8,2,1,32]{1,0,2,3,4:T(4,128)(2,1)}), bf16[4,8,2,1,32]{1,0,2,3,4:T(4,128)(2,1)S(1)}, u32[]{:S(2)}, u32[]{:S(2)}) async-start(bf16[4,8,2,1,32]{1,0,2,3,4:T(4,128)(2,1)} %copy.42), calls=%async_computation.3 | async-start | bytes 131072 | tf_op jit(solution)/shard_map/all_to_all | solution.py:116
  220.2 12.9 %all-to-all-start = ((bf16[4,8,2,1,32]{1,0,2,3,4:T(4,128)(2,1)}), bf16[4,8,2,1,32]{1,0,2,3,4:T(4,128)(2,1)S(1)}, u32[]{:S(2)}, u32[]{:S(2)}) async-start(bf16[4,8,2,1,32]{1,0,2,3,4:T(4,128)(2,1)} %copy.33), calls=%async_computation | async-start | bytes 131072 | tf_op jit(solution)/shard_map/all_to_all | solution.py:115
  235.4 12.9 %all-to-all-start.4 = ((bf16[128,8,2,1,1]{1,2,4,3,0:T(2,128)(2,1)}), bf16[128,8,2,1,1]{1,2,4,3,0:T(2,128)(2,1)S(1)}, u32[]{:S(2)}, u32[]{:S(2)}) async-start(bf16[128,8,2,1,1]{1,2,4,3,0:T(2,128)(2,1)} %copy.44), calls=%async_computation.4 | async-start | bytes 131072 | tf_op jit(solution)/shard_map/all_to_all | solution.py:148
  248.3 12.9 %all-to-all-start.1 = ((bf16[128,8,2,1,1]{1,2,4,3,0:T(2,128)(2,1)}), bf16[128,8,2,1,1]{1,2,4,3,0:T(2,128)(2,1)S(1)}, u32[]{:S(2)}, u32[]{:S(2)}) async-start(bf16[128,8,2,1,1]{1,2,4,3,0:T(2,128)(2,1)} %copy.35), calls=%async_computation.1 | async-start | bytes 131072 | tf_op jit(solution)/shard_map/all_to_all | solution.py:147
  261.2 22.5 %all-to-all-start.5 = ((bf16[16,2,768]{2,1,0:T(2,128)(2,1)}), bf16[16,2,768]{2,1,0:T(2,128)(2,1)S(1)}, u32[]{:S(2)}, u32[]{:S(2)}) async-start(bf16[16,2,768]{2,1,0:T(2,128)(2,1)} %reshape.864), calls=%async_computation.5 | async-start | bytes 98304 | tf_op jit(solution)/shard_map/all_to_all | solution.py:160
  283.8 12.5 %all-to-all-start.2 = ((bf16[16,2,768]{2,1,0:T(2,128)(2,1)}), bf16[16,2,768]{2,1,0:T(2,128)(2,1)S(1)}, u32[]{:S(2)}, u32[]{:S(2)}) async-start(bf16[16,2,768]{2,1,0:T(2,128)(2,1)} %reshape.862), calls=%async_computation.2 | async-start | bytes 98304 | tf_op jit(solution)/shard_map/all_to_all | solution.py:159
where the time goes:
time: 300 us; the launch traced here: 298 us
  blocking collectives  192 us (64%)
  starting transfers between devices  44 us (15%)
  waiting for transfers between devices  41.2 us (14%)
  local copies, waits for them, and re-layouts  10.2 us (3%)
  matrix products  6.66 us (2%)
    all_gather x1, blocking collectives, shards(): lax.all_gather(plane_f, 'space', axis=1, tiled=True)  113 us
    all_gather x1, blocking collectives, shards(): lax.all_gather(plane_g, 'space', axis=1, tiled=True)  79.5 us
    all_to_all x1, starting transfers between devices, shards(): lax.all_to_all(spread_u, 'space', split_axis=1, concat_axis=3, tiled=True)  13.5 us
    all_to_all x1, starting transfers between devices, shards(): lax.all_to_all(spec_g, 'blk', split_axis=4, concat_axis=0, tiled=True)  12.8 us
    all_to_all x1, waiting for transfers between devices, shards(): lax.all_to_all(spread_u, 'space', split_axis=1, concat_axis=3, tiled=True)  7.71 us
    all_to_all x1, waiting for transfers between devices, shards(): lax.all_to_all(spec_f, 'blk', split_axis=4, concat_axis=0, tiled=True)  7.21 us
    all_to_all x1, waiting for transfers between devices, shards(): lax.all_to_all(spread_y, 'space', split_axis=1, concat_axis=3, tiled=True)  7.14 us
    all_to_all x1, waiting for transfers between devices, shards(): lax.all_to_all(mixed, 'blk', split_axis=0, concat_axis=4, tiled=True)  6.88 us
  transfers between devices with their start and end apart: 6, of which 6 were waited for; matrix products, arithmetic and copies ran while one was open for 3% of the time, Pallas kernels for 0%

commit v1 on v0

v1 whole, which is shorter than its diff:
```python
import math

import jax
import jax.numpy as jnp
from jax import lax
from jax.sharding import PartitionSpec as P

NX = 96
NY = 192
NZ = 96
MX = 16
MY = 32
MZ = 8


def centered_freqs(total_count):
    indices = jnp.arange(total_count, dtype=jnp.int32)
    return jnp.where(indices < total_count // 2, indices, indices - total_count)


def phase_pair(frequencies, positions, length):
    product = frequencies[:, None] * positions[None, :] % length
    angles = product.astype(jnp.float32) * (2.0 * math.pi / length)
    return (jnp.cos(angles), jnp.sin(angles))


def x_analysis_table():
    cosines, sine_values = phase_pair(centered_freqs(MX), jnp.arange(NX, dtype=jnp.int32), NX)
    return jnp.stack([cosines.T, -sine_values.T], 1).astype(jnp.bfloat16)


def y_analysis_table():
    cosines, sine_values = phase_pair(centered_freqs(MY), jnp.arange(NY, dtype=jnp.int32), NY)
    real_rows = jnp.stack([cosines.T, -sine_values.T], 1)
    imag_rows = jnp.stack([sine_values.T, cosines.T], 1)
    return jnp.stack([real_rows, imag_rows], 0).astype(jnp.bfloat16)


def z_analysis_table(positions):
    cosines, sine_values = phase_pair(jnp.arange(MZ, dtype=jnp.int32), positions, NZ)
    real_rows = jnp.stack([cosines.T, -sine_values.T], 1)
    imag_rows = jnp.stack([sine_values.T, cosines.T], 1)
    return jnp.stack([real_rows, imag_rows], 0).astype(jnp.bfloat16)


def mode_weights():
    return jnp.where(jnp.arange(MZ) == 0, 1.0, 2.0).astype(jnp.float32)


def z_synthesis_table(positions, amplitude):
    cosines, sine_values = phase_pair(jnp.arange(MZ, dtype=jnp.int32), positions, NZ)
    cosines = cosines * amplitude[:, None]
    sine_values = sine_values * amplitude[:, None]
    real_rows = jnp.stack([cosines, sine_values], -1)
    imag_rows = jnp.stack([-sine_values, cosines], -1)
    return jnp.stack([real_rows, imag_rows], 1).astype(jnp.bfloat16)


def y_synthesis_table():
    cosines, sine_values = phase_pair(centered_freqs(MY), jnp.arange(NY, dtype=jnp.int32), NY)
    real_rows = jnp.stack([cosines, sine_values], 1)
    imag_rows = jnp.stack([-sine_values, cosines], 1)
    return jnp.stack([real_rows, imag_rows], 0).astype(jnp.bfloat16)


def x_synthesis_table():
    cosines, sine_values = phase_pair(centered_freqs(MX), jnp.arange(NX, dtype=jnp.int32), NX)
    return jnp.stack([cosines, -sine_values], 0).astype(jnp.bfloat16)


def contract(pattern, first_operand, second_operand):
    return jnp.einsum(pattern, first_operand, second_operand, preferred_element_type=jnp.float32)


def shards(input_field, cotangent, weights):
    forward_scale = 1.0 / math.sqrt(NX * NY * NZ)
    synth_scale = 1.0 / math.sqrt(MX * MY * MZ)
    amplitude = mode_weights()
    unit_weights = jnp.ones((MZ,), jnp.float32)
    n_space = lax.axis_size("space")
    n_blk = lax.axis_size("blk")
    chans, cells = input_field.shape[:2]
    x_table = x_analysis_table()
    y_table = y_analysis_table()

    def analyse(values):
        xsum = contract("czxy,xrp->czrpy", values, x_table).astype(jnp.bfloat16)
        return contract("czrpy,ryoq->pczoq", xsum, y_table).astype(jnp.bfloat16)

    planes = jnp.stack([analyse(input_field), analyse(cotangent)], 3)
    planes = planes.reshape(n_space, chans * cells, 2 * 2 * MY)
    planes = lax.all_to_all(planes, "space", 0, 0, tiled=True)
    planes = planes.reshape(n_space, chans, cells, 2, 2, MY)
    z_table = z_analysis_table(jnp.arange(NZ, dtype=jnp.int32))
    z_table = z_table.reshape(2, n_space, cells, 2, MZ)
    zsum = contract("sczhiq,iszok->qhcko", planes, z_table)
    scales = jnp.stack([jnp.full((MZ,), forward_scale, jnp.float32), amplitude * synth_scale])
    spec = (zsum * scales[None, :, None, :, None]).astype(jnp.bfloat16)
    spec = spec.reshape(n_blk, 1, 2 * chans * MZ * 2)
    spec = lax.all_to_all(spec, "blk", 0, 0, tiled=True)
    spec = spec.reshape(n_blk, 2, chans, MZ, 2).transpose(1, 4, 3, 0, 2).reshape(2, 2, MZ, n_blk * chans)
    f_real, f_imag = spec[0, 0], spec[0, 1]
    g_real, g_imag = spec[1, 0], spec[1, 1]
    w_real = weights[0, 0, :, 0]
    w_imag = weights[0, 0, :, 1]
    mixed_real = contract("koc,kc->ko", w_real, f_real) - contract("koc,kc->ko", w_imag, f_imag)
    mixed_imag = contract("koc,kc->ko", w_real, f_imag) + contract("koc,kc->ko", w_imag, f_real)
    grad_real = contract("koc,ko->kc", w_real, g_real) + contract("koc,ko->kc", w_imag, g_imag)
    grad_imag = contract("koc,ko->kc", w_real, g_imag) - contract("koc,ko->kc", w_imag, g_real)
    back = jnp.stack([jnp.stack([mixed_real, mixed_imag]), jnp.stack([grad_real, grad_imag])])
    back = back.astype(jnp.bfloat16).reshape(2, 2, MZ, n_blk, chans).transpose(3, 0, 4, 2, 1)
    back = back.reshape(n_blk, 1, 2 * chans * MZ * 2)
    back = lax.all_to_all(back, "blk", 0, 0, tiled=True)
    wide = jnp.float32
    fr, fi, gr, gi = (v.astype(wide) for v in (f_real, f_imag, g_real, g_imag))
    go, fc = (lambda v: v[:, :, None]), (lambda v: v[:, None, :])
    weight_grad = jnp.stack([go(gr) * fc(fr) + go(gi) * fc(fi), go(gi) * fc(fr) - go(gr) * fc(fi)], 1)[None, None]
    back = back.reshape(MY, 2, chans, MZ, 2)
    positions = jnp.arange(NZ, dtype=jnp.int32)
    tables = jnp.stack([z_synthesis_table(positions, amplitude), z_synthesis_table(positions, unit_weights)])
    tables = tables.reshape(2, MZ, 2, n_space, cells, 2)
    scales = jnp.array([synth_scale, forward_scale], jnp.float32)
    zback = jnp.einsum("qhcki,hkiszo->sqhczo", back, tables, preferred_element_type=jnp.float32)
    zback = (zback * scales[None, None, :, None, None, None]).astype(jnp.bfloat16)
    zback = zback.reshape(n_space, MY, 2 * chans * cells * 2)
    zback = lax.all_to_all(zback, "space", 0, 0, tiled=True)
    zback = zback.reshape(MX, MY, 2, chans, cells, 2)
    y_back_table = y_synthesis_table()
    x_back_table = x_synthesis_table()

    def synthesize(h):
        yback = contract("pqczi,iqoy->czopy", zback[:, :, h], y_back_table).astype(jnp.bfloat16)
        return contract("czipy,ipx->czxy", yback, x_back_table).astype(jnp.bfloat16)

    return (synthesize(0), synthesize(1), weight_grad)


def solution(mesh):
    placed = (
        P("blk", "space", None, None),
        P("blk", "space", None, None),
        P("space", "blk", None, None, None, None),
    )
    return jax.shard_map(
        shards,
        mesh=mesh,
        in_specs=placed,
        out_specs=(
            P("blk", "space", None, None),
            P("blk", "space", None, None),
            P("space", "blk", None, None, None, None),
        ),
        check_vma=False,
    )
```

time: 300 us -> 81.1 us (0.27)
  blocking collectives: 192 us -> 0 us
  starting transfers between devices: 44 us -> 31.2 us
  waiting for transfers between devices: 41.2 us -> 33.2 us
  local copies, waits for them, and re-layouts: 10.2 us -> 7 us
    all_gather x2 -> x0, blocking collectives: 192 us -> none  [the longest x1 113 us: shards(): lax.all_gather(plane_f, 'space', axis=1, tiled=True)]
    all_to_all x6 -> x4, starting transfers between devices: 44 us -> 31.2 us  [the longest x1 13.4 us: shards(): planes = lax.all_to_all(planes, 'space', 0, 0, tiled=True)]
    all_to_all x6 -> x4, waiting for transfers between devices: 41.2 us -> 33.2 us  [the longest x1 8.99 us: shards(): planes = lax.all_to_all(planes, 'space', 0, 0, tiled=True)]
    reshape x0 -> x5, local copies, waits for them, and re-layouts: none -> 3.46 us  [the longest x1 1 us: shards(): zback = zback.reshape(n_space, MY, 2 * chans * cells * 2)]
    dynamic_slice x3 -> x0, local copies, waits for them, and re-layouts: 3.39 us -> none  [the longest x2 3.1 us: shards(): lax.dynamic_slice_in_dim(pieces[1], space_index * px_local, px_local, 3)]
    dot_general x16 -> x5, matrix products: 6.66 us -> 4.47 us  [contract(): jnp.einsum(pattern, first_operand, second_operand, preferred_element_type...]
  transfers between devices with their start and end apart: 6 -> 4, of which waited for: 6 -> 4; matrix products, arithmetic and copies ran while one was open for 3% -> 3% of each run, Pallas kernels for 0% -> 0%
where the time goes in v1:
time: 81.1 us; the launch traced here: 80.7 us
  waiting for transfers between devices  33.2 us (41%)
  starting transfers between devices  31.2 us (38%)
  local copies, waits for them, and re-layouts  7 us (9%)
  matrix products  4.78 us (6%)
  other arithmetic  3.57 us (4%)
  between operations  0.94 us (1%)
    all_to_all x1, starting transfers between devices, shards(): planes = lax.all_to_all(planes, 'space', 0, 0, tiled=True)  13.4 us
    all_to_all x1, starting transfers between devices, shards(): spec = lax.all_to_all(spec, 'blk', 0, 0, tiled=True)  10 us
    all_to_all x1, waiting for transfers between devices, shards(): planes = lax.all_to_all(planes, 'space', 0, 0, tiled=True)  8.99 us
    all_to_all x1, waiting for transfers between devices, shards(): zback = lax.all_to_all(zback, 'space', 0, 0, tiled=True)  8.73 us
    all_to_all x1, waiting for transfers between devices, shards(): back = lax.all_to_all(back, 'blk', 0, 0, tiled=True)  7.84 us
    all_to_all x1, waiting for transfers between devices, shards(): spec = lax.all_to_all(spec, 'blk', 0, 0, tiled=True)  7.63 us
    dot_general x5, matrix products, contract(): jnp.einsum(pattern, first_operand, second_operand, preferred_element_type...  4.47 us
    all_to_all x1, starting transfers between devices, shards(): back = lax.all_to_all(back, 'blk', 0, 0, tiled=True)  4.28 us
  transfers between devices with their start and end apart: 4, of which 4 were waited for; matrix products, arithmetic and copies ran while one was open for 3% of the time, Pallas kernels for 0%

profile of v1, /device:TPU:1, one launch (start us, length us, event | category | flops | bytes accessed | tf_op | source)
XLA Modules:
  0.0 80.7 jit_solution(1809560388823810532)
XLA Ops:
  0.7 0.1 cosine_convert_fusion.3
  0.8 0.2 negate_convert_fusion
  1.1 0.8 %copy-done = bf16[4,6,96,192]{3,2,1,0:T(8,128)(2,1)S(1)} copy-done((bf16[4,6,96,192]{3,2,1,0:T(8,128)(2,1)S(1)}, bf16[4,6,96,192]{3,2,1,0:T(8,128)(2,1)}, u32[]{:S(2)}) %copy-start) | copy-done | bytes 884760
  1.9 0.4 fusion.15
  2.4 0.5 fusion.16
  2.9 0.4 copy.22
  3.3 0.9 %reshape.795 = bf16[16,24,128]{2,1,0:T(8,128)(2,1)} reshape(bf16[16,4,6,2,2,32]{5,4,3,2,1,0:T(2,128)(2,1)S(1)} %copy.22) | data formatting | bytes 196608 | tf_op jit(solution)/shard_map/reshape | solution.py:91
  4.2 13.4 %all-to-all-start = ((bf16[16,24,128]{2,1,0:T(8,128)(2,1)}), bf16[16,24,128]{2,1,0:T(8,128)(2,1)S(1)}, u32[]{:S(2)}, u32[]{:S(2)}) async-start(bf16[16,24,128]{2,1,0:T(8,128)(2,1)} %reshape.795), calls=%async_computation | async-start | bytes 196608 | tf_op jit(solution)/shard_map/all_to_all | solution.py:92
  17.7 0.2 fusion.69
  17.9 0.1 fusion.89
  18.2 9.0 %all-to-all-done = bf16[16,24,128]{2,1,0:T(8,128)(2,1)S(1)} async-done(((bf16[16,24,128]{2,1,0:T(8,128)(2,1)}), bf16[16,24,128]{2,1,0:T(8,128)(2,1)S(1)}, u32[]{:S(2)}, u32[]{:S(2)}) %all-to-all-start) | async-done | bytes 98336 | tf_op jit(solution)/shard_map/all_to_all | solution.py:92
  27.2 0.2 reshape.796
  27.4 0.2 fusion.18
  27.7 0.7 copy.25
  28.4 10.0 %all-to-all-start.1 = ((bf16[32,1,128]{2,1,0:T(2,128)(2,1)}), bf16[32,1,128]{2,1,0:T(2,128)(2,1)S(1)}, u32[]{:S(2)}, u32[]{:S(2)}) async-start(bf16[32,1,128]{2,1,0:T(2,128)(2,1)} %copy.25), calls=%async_computation.1 | async-start | bytes 32768 | tf_op jit(solution)/shard_map/all_to_all | solution.py:100
  38.4 0.1 cosine_convert_fusion.4
  38.5 7.6 %all-to-all-done.1 = bf16[32,1,128]{2,1,0:T(2,128)(2,1)S(1)} async-done(((bf16[32,1,128]{2,1,0:T(2,128)(2,1)}), bf16[32,1,128]{2,1,0:T(2,128)(2,1)S(1)}, u32[]{:S(2)}, u32[]{:S(2)}) %all-to-all-start.1) | async-done | bytes 8224 | tf_op jit(solution)/shard_map/all_to_all | solution.py:100
  46.3 0.1 copy.27
  46.7 0.4 fusion.29
  47.2 0.6 fusion.25
  49.0 0.7 copy.33
  49.7 4.3 %all-to-all-start.2 = ((bf16[32,1,128]{2,1,0:T(2,128)(2,1)}), bf16[32,1,128]{2,1,0:T(2,128)(2,1)S(1)}, u32[]{:S(2)}, u32[]{:S(2)}) async-start(bf16[32,1,128]{2,1,0:T(2,128)(2,1)} %copy.33), calls=%async_computation.2 | async-start | bytes 32768 | tf_op jit(solution)/shard_map/all_to_all | solution.py:113
  54.0 7.8 %all-to-all-done.2 = bf16[32,1,128]{2,1,0:T(2,128)(2,1)S(1)} async-done(((bf16[32,1,128]{2,1,0:T(2,128)(2,1)}), bf16[32,1,128]{2,1,0:T(2,128)(2,1)S(1)}, u32[]{:S(2)}, u32[]{:S(2)}) %all-to-all-start.2) | async-done | bytes 8224 | tf_op jit(solution)/shard_map/all_to_all | solution.py:113
  62.0 0.3 fusion.10
  62.4 1.0 %copy.37 = bf16[16,32,96]{2,1,0:T(8,128)(2,1)} copy(bf16[16,32,96]{1,0,2:T(8,128)(2,1)S(1)} %bitcast.229) | data formatting | bytes 196608 | tf_op jit(solution)/shard_map/reshape | solution.py:125
  63.4 3.5 %all-to-all-start.3 = ((bf16[16,32,96]{2,1,0:T(8,128)(2,1)}), bf16[16,32,96]{2,1,0:T(8,128)(2,1)S(1)}, u32[]{:S(2)}, u32[]{:S(2)}) async-start(bf16[16,32,96]{2,1,0:T(8,128)(2,1)} %copy.37), calls=%async_computation.3 | async-start | bytes 262144 | tf_op jit(solution)/shard_map/all_to_all | solution.py:126
  66.9 0.3 multiply_add_fusion
  67.2 1.1 %maximum_bitcast_fusion = f32[1,1,8,2,128,128]{5,4,3,2,1,0:T(8,128)} fusion(f32[8,1,128,128]{3,2,1,0:T(8,128)S(1)} %get-tuple-element.20, f32[8,1,128,128]{3,2,1,0:T(8,128)S(1)} %get-tuple-element.19), kind=kLoop, calls=%fused_computation.29 | loop fusion | flops 262144 | bytes 2097152 | tf_op jit(solution)/shard_map/broadcast_in_dim | solution.py:117
  68.3 8.7 %all-to-all-done.3 = bf16[16,32,96]{2,1,0:T(8,128)(2,1)S(1)} async-done(((bf16[16,32,96]{2,1,0:T(8,128)(2,1)}), bf16[16,32,96]{2,1,0:T(8,128)(2,1)S(1)}, u32[]{:S(2)}, u32[]{:S(2)}) %all-to-all-start.3) | async-done | bytes 98336 | tf_op jit(solution)/shard_map/all_to_all | solution.py:126
  77.0 0.3 copy.38
  77.4 1.7 %fusion.1 = bf16[4,6,96,192]{3,2,1,0:T(8,128)(2,1)} fusion(bf16[16,32,2,4,6,2]{1,0,5,4,3,2:T(8,128)(2,1)S(1)} %bitcast.230, bf16[1,32,2,192]{3,1,0,2:T(8,128)(2,1)S(1)} %get-tuple-element.22, bf16[1,32,2,192]{3,1,0,2:T(8,128)(2,1)S(1)} %get-tuple-element.21, bf16[1,16,96]{2,1,0:T(8,128)(2,1)S(1)} %get-tuple-element.35, ...), kind=kOutput, calls=%fused_computation.3 | convolution fusion | flops 47886336 | bytes 1155072 | tf_op jit(solution)/shard_map/czipy,ipx->czxy/dot_general | solution.py:72
  79.0 1.7 %fusion = bf16[4,6,96,192]{3,2,1,0:T(8,128)(2,1)} fusion(bf16[16,32,2,4,6,2]{1,0,5,4,3,2:T(8,128)(2,1)S(1)} %bitcast.231, bf16[1,32,2,192]{3,1,0,2:T(8,128)(2,1)S(1)} %get-tuple-element.22, bf16[1,32,2,192]{3,1,0,2:T(8,128)(2,1)S(1)} %get-tuple-element.21, bf16[1,16,96]{2,1,0:T(8,128)(2,1)S(1)} %get-tuple-element.35, ...), kind=kOutput, calls=%fused_computation.2 | convolution fusion | flops 47886336 | bytes 1155072 | tf_op jit(solution)/shard_map/czipy,ipx->czxy/dot_general | solution.py:72
  (44 shorter events, 2.1 us)
Async XLA Ops:
  0.6 1.3 %copy-start = (bf16[4,6,96,192]{3,2,1,0:T(8,128)(2,1)S(1)}, bf16[4,6,96,192]{3,2,1,0:T(8,128)(2,1)}, u32[]{:S(2)}) copy-start(bf16[4,6,96,192]{3,2,1,0:T(8,128)(2,1)} %param.5) | copy-start | bytes 2654212
  0.6 1.7 %copy-start.2 = (bf16[4,6,96,192]{3,2,1,0:T(8,128)(2,1)S(1)}, bf16[4,6,96,192]{3,2,1,0:T(8,128)(2,1)}, u32[]{:S(2)}) copy-start(bf16[4,6,96,192]{3,2,1,0:T(8,128)(2,1)} %param.4) | copy-start | bytes 2654212
  4.2 23.0 %all-to-all-start = ((bf16[16,24,128]{2,1,0:T(8,128)(2,1)}), bf16[16,24,128]{2,1,0:T(8,128)(2,1)S(1)}, u32[]{:S(2)}, u32[]{:S(2)}) async-start(bf16[16,24,128]{2,1,0:T(8,128)(2,1)} %reshape.795), calls=%async_computation | async-start | bytes 196608 | tf_op jit(solution)/shard_map/all_to_all | solution.py:92
  18.0 28.7 %copy-start.1 = (bf16[1,1,8,2,128,128]{5,4,3,2,1,0:T(8,128)(2,1)S(1)}, bf16[1,1,8,2,128,128]{5,4,3,2,1,0:T(8,128)(2,1)}, u32[]{:S(2)}) copy-start(bf16[1,1,8,2,128,128]{5,4,3,2,1,0:T(8,128)(2,1)} %param.6) | copy-start | bytes 1572868
  28.4 17.8 %all-to-all-start.1 = ((bf16[32,1,128]{2,1,0:T(2,128)(2,1)}), bf16[32,1,128]{2,1,0:T(2,128)(2,1)S(1)}, u32[]{:S(2)}, u32[]{:S(2)}) async-start(bf16[32,1,128]{2,1,0:T(2,128)(2,1)} %copy.25), calls=%async_computation.1 | async-start | bytes 32768 | tf_op jit(solution)/shard_map/all_to_all | solution.py:100
  47.1 14.9 %copy-start.3 = (f32[2]{0:T(128)S(1)}, f32[2]{0:T(128)}, u32[]{:S(2)}) copy-start(f32[2]{0:T(128)} %constant.80.clone) | copy-start | bytes 28
  49.7 12.2 %all-to-all-start.2 = ((bf16[32,1,128]{2,1,0:T(2,128)(2,1)}), bf16[32,1,128]{2,1,0:T(2,128)(2,1)S(1)}, u32[]{:S(2)}, u32[]{:S(2)}) async-start(bf16[32,1,128]{2,1,0:T(2,128)(2,1)} %copy.33), calls=%async_computation.2 | async-start | bytes 32768 | tf_op jit(solution)/shard_map/all_to_all | solution.py:113
  63.4 13.7 %all-to-all-start.3 = ((bf16[16,32,96]{2,1,0:T(8,128)(2,1)}), bf16[16,32,96]{2,1,0:T(8,128)(2,1)S(1)}, u32[]{:S(2)}, u32[]{:S(2)}) async-start(bf16[16,32,96]{2,1,0:T(8,128)(2,1)} %copy.37), calls=%async_computation.3 | async-start | bytes 262144 | tf_op jit(solution)/shard_map/all_to_all | solution.py:126

commit v2 on v1

v2 whole, which is shorter than its diff:
```python
import math

import jax
import jax.numpy as jnp
import numpy as np
from jax import lax
from jax.experimental import pallas as pl
from jax.experimental.pallas import tpu as pltpu
from jax.sharding import PartitionSpec as P

NX = 96
NY = 192
NZ = 96
MX = 16
MY = 32
MZ = 8
CHANS = 4
CELLS = 6
N_SPACE = 16
N_BLK = 32
PAIR = 2
N_LINE = N_BLK // PAIR
QS = MY // PAIR
ROWS = 16
USED = CHANS // 2 * CELLS
LANES = 128
HALF = LANES // 2
MODES = PAIR * 2 * MZ
FORWARD = 1.0 / math.sqrt(NX * NY * NZ)
SYNTH = 1.0 / math.sqrt(MX * MY * MZ)
VMEM_LIMIT = 48 * 1024 * 1024
ALL_VMEM = 63 * 1024 * 1024
F32 = jnp.float32
BF16 = jnp.bfloat16


def freqs(count):
    index = np.arange(count)
    return np.where(index < count // 2, index, index - count)


def phases(frequencies, length):
    product = (frequencies[:, None] * np.arange(length)[None, :]) % length
    angles = product.astype(np.float32) * np.float32(2.0 * math.pi / length)
    return np.cos(angles).astype(np.float32), np.sin(angles).astype(np.float32)


def bf16(table):
    return jnp.asarray(table.astype(BF16))


def y_analysis():
    cosines, sines = (v.T.reshape(NY, PAIR, QS) for v in phases(freqs(MY), NY))
    table = np.zeros((2, NY, 2, PAIR, 2, 2, QS), np.float32)
    for h in range(2):
        table[h, :, 0, :, h, 0] = cosines
        table[h, :, 0, :, h, 1] = -sines
        table[h, :, 1, :, h, 0] = -sines
        table[h, :, 1, :, h, 1] = -cosines
    return bf16(table.reshape(2, NY, 2 * LANES))


def x_analysis():
    cosines, sines = phases(freqs(MX), NX)
    return bf16(np.concatenate([cosines, sines], 0))


def z_table():
    cosines, sines = (v.reshape(MZ, N_SPACE, CELLS) for v in phases(np.arange(MZ), NZ))
    table = np.zeros((2, PAIR, 2, MZ, PAIR, N_SPACE, ROWS), np.float32)
    for pair in range(PAIR):
        for cl in range(2):
            cells = slice(cl * CELLS, (cl + 1) * CELLS)
            table[0, pair, cl, :, pair, :, cells] = cosines
            table[1, pair, cl, :, pair, :, cells] = sines
    return table.reshape(2 * MODES, PAIR * N_SPACE * ROWS)


def x_synthesis():
    cosines, sines = phases(freqs(MX), NX)
    return bf16(np.concatenate([cosines.T, sines.T], 1))


def y_synthesis():
    cosines, sines = (v.reshape(PAIR, QS, NY) for v in phases(freqs(MY), NY))
    table = np.zeros((2, PAIR, 2, 2, QS, NY), np.float32)
    for h in range(2):
        table[h, :, h, 0] = cosines
        table[h, :, h, 1] = -sines
    return bf16(table.reshape(2, LANES, NY))


def dot(a, b):
    return jnp.dot(a, b, preferred_element_type=F32)


def dot_first(a, b):
    return lax.dot_general(a, b, (((0,), (0,)), ((), ())), preferred_element_type=F32)


def dot_last(a, b):
    return lax.dot_general(a, b, (((1,), (1,)), ((), ())), preferred_element_type=F32)


def index(shape, dim):
    return lax.broadcasted_iota(jnp.int32, shape, dim)


def times_minus_i(a):
    real = index(a.shape, 1) // QS % 2 == 0
    return jnp.where(real, pltpu.roll(a, LANES - QS, 1), -pltpu.roll(a, QS, 1))


def times_i(a):
    real = index(a.shape, 1) // QS % 2 == 0
    return jnp.where(real, -pltpu.roll(a, LANES - QS, 1), pltpu.roll(a, QS, 1))


def low_halves(a, b):
    return jnp.where(index(a.shape, 1) < HALF, a, pltpu.roll(b, HALF, 1))


def high_halves(a, b):
    return jnp.where(index(a.shape, 1) < HALF, pltpu.roll(a, HALF, 1), b)


def analyse_kernel(f_hbm, g_hbm, y_hbm, x_hbm, out_ref, f_ref, g_ref, y_ref, x_ref, planes, sems):
    copies = [
        pltpu.make_async_copy(y_hbm, y_ref, sems.at[0]),
        pltpu.make_async_copy(x_hbm, x_ref, sems.at[1]),
    ]
    for c in range(CHANS):
        copies.append(pltpu.make_async_copy(f_hbm.at[c], f_ref.at[c], sems.at[2 + 2 * c]))
        copies.append(pltpu.make_async_copy(g_hbm.at[c], g_ref.at[c], sems.at[3 + 2 * c]))
    for copy in copies:
        copy.start()
    for ch in range(2):
        start = (ch * ROWS + USED) * MX
        planes[start : start + (ROWS - USED) * MX, :] = jnp.zeros(((ROWS - USED) * MX, LANES), F32)
    rows = CELLS * NX
    copies[0].wait()
    copies[1].wait()
    for c in range(CHANS):
        copies[2 + 2 * c].wait()
        copies[3 + 2 * c].wait()
        both = dot(f_ref[c].reshape(rows, NY), y_ref[0]) + dot(g_ref[c].reshape(rows, NY), y_ref[1])
        both = both.astype(BF16)
        for z in range(CELLS):
            part = dot(x_ref[...], both[z * NX : (z + 1) * NX])
            start = (c // 2 * ROWS + c % 2 * CELLS + z) * MX
            planes[start : start + MX, :] = part[:MX, :LANES] + part[MX:, LANES:]
    for p in range(MX):
        first = planes[pl.ds(p, ROWS, stride=MX), :]
        second = planes[pl.ds(ROWS * MX + p, ROWS, stride=MX), :]
        out_ref[p] = low_halves(first, second).astype(BF16)
        out_ref[N_SPACE + p] = high_halves(first, second).astype(BF16)


def message():
    return jax.ShapeDtypeStruct((PAIR * N_SPACE, ROWS, LANES), BF16)


def field_buffer():
    return pltpu.VMEM((CHANS, CELLS, NX, NY), BF16)


def call(kernel, name, out_shape, *operands, in_specs=None, out_specs=None, scratch=(), vmem=VMEM_LIMIT):
    whole = pl.BlockSpec(memory_space=pltpu.VMEM)
    return pl.pallas_call(
        kernel,
        in_specs=in_specs or [whole] * len(operands),
        out_specs=out_specs or jax.tree.map(lambda _: whole, out_shape),
        out_shape=out_shape,
        scratch_shapes=list(scratch),
        compiler_params=pltpu.CompilerParams(vmem_limit_bytes=vmem),
        name=name,
    )(*operands)


def analyse(field, cotangent):
    return call(
        analyse_kernel,
        "analyse",
        message(),
        field,
        cotangent,
        y_analysis(),
        x_analysis(),
        in_specs=[pl.BlockSpec(memory_space=pltpu.HBM)] * 4,
        scratch=[
            field_buffer(),
            field_buffer(),
            pltpu.VMEM((2, NY, 2 * LANES), BF16),
            pltpu.VMEM((2 * MX, NX), BF16),
            pltpu.VMEM((2 * ROWS * MX, LANES), F32),
            pltpu.SemaphoreType.DMA((2 + 2 * CHANS,)),
        ],
        vmem=ALL_VMEM,
    )


def mode_picker(ch):
    shape = (2 * QS, LANES)
    row, lane = index(shape, 0), index(shape, 1)
    return jnp.where(row == lane % QS * 2 + ch, 1.0, 0.0).astype(BF16)


def channel_picker():
    shape = (2 * N_LINE, LANES)
    row, lane = index(shape, 0), index(shape, 1)
    return jnp.where(row == lane // 4 % N_LINE * 2 + lane // 2 % 2, 1.0, 0.0).astype(BF16)


def channel_part(shape):
    lane = index(shape, len(shape) - 1)
    return lane // HALF * 2 + lane % 2


def sum_z_kernel(planes_ref, z_ref, out_ref):
    planes = planes_ref[...].reshape(PAIR * N_SPACE * ROWS, LANES)
    sums = dot(z_ref[...], planes)
    spec = sums[:MODES] + times_minus_i(sums[MODES:])
    field = index(spec.shape, 1) // (2 * QS) % 2
    zero = index(spec.shape, 0) % MZ == 0
    scale = jnp.where(field == 0, FORWARD, jnp.where(zero, SYNTH, 2.0 * SYNTH))
    spec = (spec * scale.astype(F32)).astype(BF16).astype(F32)
    shape = (8, MODES, LANES)
    spread = jnp.where(index(shape, 2) // QS == index(shape, 0), spec[None], 0.0).astype(BF16)
    spread = spread.reshape(8 * MODES, LANES)
    first, second = spread[:LANES], spread[LANES:]
    out_ref[...] = dot_last(mode_picker(0), first) + dot_last(mode_picker(1), second)


def mix_kernel(spec_ref, w_ref, back_ref, chan_ref):
    pick = channel_picker()
    wide = dot_first(spec_ref[...].astype(BF16), pick).reshape(4, 4, MZ, LANES)
    part = channel_part((4, MZ, LANES))
    spec = wide[:, 0]
    for j in range(1, 4):
        spec = jnp.where(part == j, wide[:, j], spec)
    chan_ref[...] = spec.reshape(4 * MZ, LANES)
    fr, fi, gr, gi = (spec[i] for i in range(4))
    f = jnp.concatenate([fr, fi], 0).astype(BF16)
    f_turned = jnp.concatenate([-fi, fr], 0).astype(BF16)
    g = jnp.concatenate([gr, gi], 0).astype(BF16)
    g_turned = jnp.concatenate([gi, -gr], 0).astype(BF16)
    own = index((2 * MZ, LANES), 0) % MZ
    mixed = jnp.zeros((2 * MZ, LANES), F32)
    grad = jnp.zeros((2 * MZ, LANES), F32)
    for k in range(MZ):
        w_real = w_ref[0, 0, k, 0]
        w_imag = w_ref[0, 0, k, 1]
        mixed = jnp.where(own == k, dot_last(f, w_real) + dot_last(f_turned, w_imag), mixed)
        grad = jnp.where(own == k, dot(g, w_real) + dot(g_turned, w_imag), grad)
    back = jnp.concatenate([mixed, grad], 0).reshape(4, 1, MZ, LANES)
    shape = (4, 4, MZ, LANES)
    spread = jnp.where(channel_part(shape) == index(shape, 1), back, 0.0).astype(BF16)
    back_ref[...] = dot_last(pick, spread.reshape(LANES, LANES))


def spread_z_kernel(back_ref, z_ref, out_ref):
    back = back_ref[...].astype(BF16)
    owner = index((MODES, LANES), 1) // QS
    spec = jnp.zeros((MODES, LANES), F32)
    for ch in range(2):
        wide = dot_first(back, mode_picker(ch)).reshape(4, MODES, LANES)
        for part in range(4):
            spec = jnp.where(owner == 4 * ch + part, wide[part], spec)
    field = owner // 2 % 2
    zero = index(spec.shape, 0) % MZ == 0
    spec = jnp.where((field == 0) & ~zero, 2.0 * spec, spec)
    stacked = jnp.concatenate([spec, times_i(spec)], 0).astype(BF16)
    lane = index((1, LANES), 1) // (2 * QS) % 2
    scale = jnp.where(lane == 0, SYNTH, FORWARD).astype(F32)
    zback = (dot(z_ref[...], stacked) * scale).astype(BF16)
    out_ref[...] = zback.reshape(PAIR * N_SPACE, ROWS, LANES)


def synthesize_kernel(zback_ref, x_ref, y_ref, out_hbm, grad_hbm, out_ref, grad_ref, planes, sems):
    planes[...] = zback_ref[...].astype(F32).reshape(PAIR * N_SPACE * ROWS, LANES)
    copies = []
    for c in range(CHANS):
        parts = []
        for z in range(CELLS):
            row = c % 2 * CELLS + z
            first = planes[pl.ds(row, MX, stride=ROWS), :]
            second = planes[pl.ds(MX * ROWS + row, MX, stride=ROWS), :]
            plane = low_halves(first, second) if c < 2 else high_halves(first, second)
            stacked = jnp.concatenate([plane, times_i(plane)], 0).astype(BF16)
            parts.append(dot(x_ref[...], stacked).astype(BF16))
        both = jnp.concatenate(parts, 0)
        for i, (buffer, target) in enumerate(((out_ref, out_hbm), (grad_ref, grad_hbm))):
            buffer[c] = dot(both, y_ref[i]).astype(BF16).reshape(CELLS, NX, NY)
            copy = pltpu.make_async_copy(buffer.at[c], target.at[c], sems.at[2 * c + i])
            copy.start()
            copies.append(copy)
    for copy in copies:
        copy.wait()


def synthesize(zback):
    shape = jax.ShapeDtypeStruct((CHANS, CELLS, NX, NY), BF16)
    return call(
        synthesize_kernel,
        "synthesize",
        (shape, shape),
        zback,
        x_synthesis(),
        y_synthesis(),
        out_specs=(pl.BlockSpec(memory_space=pltpu.HBM),) * 2,
        scratch=[
            field_buffer(),
            field_buffer(),
            pltpu.VMEM((PAIR * N_SPACE * ROWS, LANES), F32),
            pltpu.SemaphoreType.DMA((2 * CHANS,)),
        ],
    )


def outer(values):
    groups = [
        [(pair * N_LINE + line) * N_SPACE + s for pair in range(PAIR) for s in range(N_SPACE)]
        for line in range(N_LINE)
    ]
    return lax.all_to_all(values, ("blk", "space"), 0, 0, tiled=True, axis_index_groups=groups)


def inner(values):
    groups = [[pair * N_LINE + line for line in range(N_LINE)] for pair in range(PAIR)]
    values = values.reshape(N_LINE, 2, LANES)
    values = lax.all_to_all(values, "blk", 0, 0, tiled=True, axis_index_groups=groups)
    return values.reshape(2 * N_LINE, LANES)


def shards(input_field, cotangent, weights):
    planes = outer(analyse(input_field, cotangent))
    small = jax.ShapeDtypeStruct((2 * N_LINE, LANES), F32)
    table = z_table()
    spec = inner(call(sum_z_kernel, "sum_z", small, planes, bf16(table)))
    back, chan = call(mix_kernel, "mix", (small, small), spec, weights)
    back = inner(back)
    fr, fi, gr, gi = (chan[i * MZ : (i + 1) * MZ] for i in range(4))
    go, fc = (lambda v: v[:, :, None]), (lambda v: v[:, None, :])
    weight_grad = jnp.stack([go(gr) * fc(fr) + go(gi) * fc(fi), go(gi) * fc(fr) - go(gr) * fc(fi)], 1)[None, None]
    zback = outer(call(spread_z_kernel, "spread_z", message(), back, bf16(table.T)))
    spectral_out, field_grad = synthesize(zback)
    return (spectral_out, field_grad, weight_grad)


def solution(mesh):
    fields = P("blk", "space", None, None)
    modes = P("space", "blk", None, None, None, None)
    return jax.shard_map(
        shards,
        mesh=mesh,
        in_specs=(fields, fields, modes),
        out_specs=(fields, fields, modes),
        check_vma=False,
    )
```

time: 81.1 us -> 74.3 us (0.916)
  blocking collectives: 0 us -> 39.4 us
  starting transfers between devices: 31.2 us -> 7.54 us
  waiting for transfers between devices: 33.2 us -> 15.2 us
  Pallas kernels: 0 us -> 9.65 us
  local copies, waits for them, and re-layouts: 7 us -> 0.03 us
  matrix products: 4.78 us -> 0 us
  other arithmetic: 3.57 us -> 1.41 us
    all_to_all x0 -> x2, blocking collectives: none -> 39.4 us  [the longest x1 23 us: outer(): lax.all_to_all(values, ('blk', 'space'), 0, 0, tiled=True, axis_index_gro...]
    all_to_all x4 -> x2, starting transfers between devices: 31.2 us -> 7.54 us  [the longest x1 3.86 us: outer(): lax.all_to_all(values, ('blk', 'space'), 0, 0, tiled=True, axis_index_gro...]
    all_to_all x4 -> x2, waiting for transfers between devices: 33.2 us -> 15.2 us  [the longest x1 7.78 us: outer(): lax.all_to_all(values, ('blk', 'space'), 0, 0, tiled=True, axis_index_gro...]
    pallas_call x0 -> x5, Pallas kernels: none -> 9.65 us  [call(): pl.pallas_call(kernel, in_specs=in_specs or [whole] * len(operands), out_...]
    dot_general x6 -> x0, matrix products: 4.78 us -> none  [the longest x5 4.47 us: contract(): jnp.einsum(pattern, first_operand, second_operand, preferred_element_type...]
    reshape x5 -> x0, local copies, waits for them, and re-layouts: 3.46 us -> none  [the longest x1 1 us: shards(): zback = zback.reshape(n_space, MY, 2 * chans * cells * 2)]
    another operation x13 -> x0, other arithmetic: 1.11 us -> none
    unnamed x12 -> x10, local copies, waits for them, and re-layouts: 1.12 us -> 0.03 us
  transfers between devices with their start and end apart: 4 -> 2, of which waited for: 4 -> 2; matrix products, arithmetic and copies ran while one was open for 3% -> 2% of each run, Pallas kernels for 0% -> 0%
where the time goes in v2:
time: 74.3 us; the launch traced here: 74 us
  blocking collectives  39.4 us (53%)
  waiting for transfers between devices  15.2 us (20%)
  Pallas kernels  9.65 us (13%)
  starting transfers between devices  7.54 us (10%)
  other arithmetic  1.41 us (2%)
    all_to_all x1, blocking collectives, outer(): lax.all_to_all(values, ('blk', 'space'), 0, 0, tiled=True, axis_index_gro...  23 us
    all_to_all x1, blocking collectives, inner(): lax.all_to_all(values, 'blk', 0, 0, tiled=True, axis_index_groups=groups)  16.4 us
    pallas_call x5, Pallas kernels, call(): pl.pallas_call(kernel, in_specs=in_specs or [whole] * len(operands), out_...  9.65 us
    all_to_all x1, waiting for transfers between devices, outer(): lax.all_to_all(values, ('blk', 'space'), 0, 0, tiled=True, axis_index_gro...  7.78 us
    all_to_all x1, waiting for transfers between devices, inner(): lax.all_to_all(values, 'blk', 0, 0, tiled=True, axis_index_groups=groups)  7.41 us
    all_to_all x1, starting transfers between devices, outer(): lax.all_to_all(values, ('blk', 'space'), 0, 0, tiled=True, axis_index_gro...  3.86 us
    all_to_all x1, starting transfers between devices, inner(): lax.all_to_all(values, 'blk', 0, 0, tiled=True, axis_index_groups=groups)  3.68 us
  transfers between devices with their start and end apart: 2, of which 2 were waited for; matrix products, arithmetic and copies ran while one was open for 2% of the time, Pallas kernels for 0%

profile of v2, /device:TPU:1, one launch (start us, length us, event | category | flops | bytes accessed | tf_op | source)
XLA Modules:
  0.0 74.0 jit_solution(17677400335936543998)
XLA Ops:
  0.6 0.0 copy-start.3
  0.6 0.0 copy-start
  0.7 4.4 %analyse.1 = bf16[32,16,128]{2,1,0:T(8,128)(2,1)} custom-call(bf16[4,6,96,192]{3,2,1,0:T(8,128)(2,1)} %f_hbm.1, bf16[4,6,96,192]{3,2,1,0:T(8,128)(2,1)} %g_hbm.1, bf16[2,192,256]{2,1,0:T(8,128)(2,1)} %constant.12.clone.y_hbm, bf16[32,96]{1,0:T(8,128)(2,1)} %constant.13.clone.x_hbm), custom_call_target="tpu_custom_call" | custom-call | tf_op jit(solution)/shard_map/analyse/pallas_call | solution.py:169
  5.0 0.0 copy-start.2
  5.0 23.0 %all_to_all.20.planes_ref = bf16[32,16,128]{2,1,0:T(8,128)(2,1)S(1)} all-to-all(bf16[32,16,128]{2,1,0:T(8,128)(2,1)} %analyse.1), channel_id=1, replica_groups={{0,1,2,3,4,5,6,7,8,9,10,11,12,13,14,15,256,257,258,259,260,261,262,263,..., dimensions={0} | all-to-all | bytes 262144 | tf_op jit(solution)/shard_map/all_to_all | solution.py:325
  28.1 0.0 copy-done.3
  28.1 0.4 sum_z.1
  28.4 16.4 %all_to_all.21 = f32[16,2,128]{2,1,0:T(2,128)S(1)} all-to-all(f32[16,2,128]{2,1,0:T(2,128)S(1)} %bitcast.8), channel_id=1, replica_groups={{0,16,32,48,64,80,96,112,128,144,160,176,192,208,224,240},{256,272,288,..., dimensions={0} | all-to-all | bytes 32768 | tf_op jit(solution)/shard_map/all_to_all | solution.py:331
  44.8 0.0 copy-done
  44.8 1.5 %mix.1 = (f32[32,128]{1,0:T(8,128)}, f32[32,128]{1,0:T(8,128)S(1)}) custom-call(f32[32,128]{1,0:T(8,128)S(1)} %bitcast.7, bf16[1,1,8,2,128,128]{5,4,3,2,1,0:T(8,128)(2,1)S(1)} %copy-done), custom_call_target="tpu_custom_call" | custom-call | tf_op jit(solution)/shard_map/mix/pallas_call | solution.py:169
  46.3 3.7 %all-to-all-start.2 = ((f32[16,2,128]{2,1,0:T(2,128)}), f32[16,2,128]{2,1,0:T(2,128)S(1)}, u32[]{:S(2)}, u32[]{:S(2)}) async-start(f32[16,2,128]{2,1,0:T(2,128)} %bitcast.2), calls=%async_computation.2 | async-start | bytes 32768 | tf_op jit(solution)/shard_map/all_to_all | solution.py:331
  50.0 7.4 %all-to-all-done.2 = f32[16,2,128]{2,1,0:T(2,128)S(1)} async-done(((f32[16,2,128]{2,1,0:T(2,128)}), f32[16,2,128]{2,1,0:T(2,128)S(1)}, u32[]{:S(2)}, u32[]{:S(2)}) %all-to-all-start.2) | async-done | bytes 16416 | tf_op jit(solution)/shard_map/all_to_all | solution.py:331
  57.4 0.0 copy-done.2
  57.4 1.1 %spread_z.1 = bf16[32,16,128]{2,1,0:T(8,128)(2,1)} custom-call(f32[32,128]{1,0:T(8,128)S(1)} %bitcast.6, bf16[512,64]{1,0:T(8,128)(2,1)S(1)} %copy-done.2), custom_call_target="tpu_custom_call" | custom-call | tf_op jit(solution)/shard_map/spread_z/pallas_call | solution.py:169
  58.5 3.9 %all-to-all-start.3 = ((bf16[32,16,128]{2,1,0:T(8,128)(2,1)}), bf16[32,16,128]{2,1,0:T(8,128)(2,1)S(1)}, u32[]{:S(2)}, u32[]{:S(2)}) async-start(bf16[32,16,128]{2,1,0:T(8,128)(2,1)} %spread_z.1), calls=%async_computation.3 | async-start | bytes 262144 | tf_op jit(solution)/shard_map/all_to_all | solution.py:325
  62.4 0.3 multiply_add_fusion
  62.7 0.0 copy-start.1
  62.7 0.0 copy-start.4
  62.7 1.1 %maximum_bitcast_fusion = f32[1,1,8,2,128,128]{5,4,3,2,1,0:T(8,128)} fusion(f32[8,1,128,128]{3,2,1,0:T(8,128)S(1)} %get-tuple-element.12, f32[8,1,128,128]{3,2,1,0:T(8,128)S(1)} %get-tuple-element.11), kind=kLoop, calls=%fused_computation | loop fusion | flops 262144 | bytes 2097152 | tf_op jit(solution)/shard_map/broadcast_in_dim | solution.py:344
  63.8 7.8 %all-to-all-done.3.zback_ref = bf16[32,16,128]{2,1,0:T(8,128)(2,1)S(1)} async-done(((bf16[32,16,128]{2,1,0:T(8,128)(2,1)}), bf16[32,16,128]{2,1,0:T(8,128)(2,1)S(1)}, u32[]{:S(2)}, u32[]{:S(2)}) %all-to-all-start.3) | async-done | bytes 131104 | tf_op jit(solution)/shard_map/all_to_all | solution.py:325
  71.6 0.0 copy-done.1
  71.6 0.0 copy-done.4
  71.6 2.4 %synthesize.1 = (bf16[4,6,96,192]{3,2,1,0:T(8,128)(2,1)}, bf16[4,6,96,192]{3,2,1,0:T(8,128)(2,1)}) custom-call(bf16[32,16,128]{2,1,0:T(8,128)(2,1)S(1)} %all-to-all-done.3.zback_ref, bf16[96,32]{1,0:T(8,128)(2,1)S(1)} %copy-done.4, bf16[2,128,192]{2,1,0:T(8,128)(2,1)S(1)} %copy-done.1), custom_call_target="tpu_custom_call" | custom-call | tf_op jit(solution)/shard_map/synthesize/pallas_call | solution.py:169
  (1 shorter events, 0.0 us)
Async XLA Ops:
  0.6 27.4 %copy-start.3 = (bf16[64,512]{1,0:T(8,128)(2,1)S(1)}, bf16[64,512]{1,0:T(8,128)(2,1)}, u32[]{:S(2)}) copy-start(bf16[64,512]{1,0:T(8,128)(2,1)} %constant.14.clone.z_ref) | copy-start | bytes 196612
  0.6 44.2 %copy-start = (bf16[1,1,8,2,128,128]{5,4,3,2,1,0:T(8,128)(2,1)S(1)}, bf16[1,1,8,2,128,128]{5,4,3,2,1,0:T(8,128)(2,1)}, u32[]{:S(2)}) copy-start(bf16[1,1,8,2,128,128]{5,4,3,2,1,0:T(8,128)(2,1)} %w_ref.1) | copy-start | bytes 1572868
  5.0 52.4 %copy-start.2 = (bf16[512,64]{1,0:T(8,128)(2,1)S(1)}, bf16[512,64]{1,0:T(8,128)(2,1)}, u32[]{:S(2)}) copy-start(bf16[512,64]{1,0:T(8,128)(2,1)} %constant.15.clone.z_ref) | copy-start | bytes 196612
  46.3 11.1 %all-to-all-start.2 = ((f32[16,2,128]{2,1,0:T(2,128)}), f32[16,2,128]{2,1,0:T(2,128)S(1)}, u32[]{:S(2)}, u32[]{:S(2)}) async-start(f32[16,2,128]{2,1,0:T(2,128)} %bitcast.2), calls=%async_computation.2 | async-start | bytes 32768 | tf_op jit(solution)/shard_map/all_to_all | solution.py:331
  58.5 13.1 %all-to-all-start.3 = ((bf16[32,16,128]{2,1,0:T(8,128)(2,1)}), bf16[32,16,128]{2,1,0:T(8,128)(2,1)S(1)}, u32[]{:S(2)}, u32[]{:S(2)}) async-start(bf16[32,16,128]{2,1,0:T(8,128)(2,1)} %spread_z.1), calls=%async_computation.3 | async-start | bytes 262144 | tf_op jit(solution)/shard_map/all_to_all | solution.py:325
  62.7 8.9 %copy-start.1 = (bf16[2,128,192]{2,1,0:T(8,128)(2,1)S(1)}, bf16[2,128,192]{2,1,0:T(8,128)(2,1)}, u32[]{:S(2)}) copy-start(bf16[2,128,192]{2,1,0:T(8,128)(2,1)} %constant.17.clone.y_ref) | copy-start | bytes 294916
  62.7 8.9 %copy-start.4 = (bf16[96,32]{1,0:T(8,128)(2,1)S(1)}, bf16[96,32]{1,0:T(8,128)(2,1)}, u32[]{:S(2)}) copy-start(bf16[96,32]{1,0:T(8,128)(2,1)} %constant.16.clone.x_ref) | copy-start | bytes 18436

commit v3 on v2

--- a/solution.py
+++ b/solution.py
@@ -29,7 +29,6 @@
 FORWARD = 1.0 / math.sqrt(NX * NY * NZ)
 SYNTH = 1.0 / math.sqrt(MX * MY * MZ)
 VMEM_LIMIT = 48 * 1024 * 1024
-ALL_VMEM = 63 * 1024 * 1024
 F32 = jnp.float32
 BF16 = jnp.bfloat16
 
@@ -51,13 +50,13 @@
 
 def y_analysis():
     cosines, sines = (v.T.reshape(NY, PAIR, QS) for v in phases(freqs(MY), NY))
-    table = np.zeros((2, NY, 2, PAIR, 2, 2, QS), np.float32)
+    table = np.zeros((2, 2, NY, PAIR, 2, 2, QS), np.float32)
     for h in range(2):
-        table[h, :, 0, :, h, 0] = cosines
-        table[h, :, 0, :, h, 1] = -sines
-        table[h, :, 1, :, h, 0] = -sines
-        table[h, :, 1, :, h, 1] = -cosines
-    return bf16(table.reshape(2, NY, 2 * LANES))
+        table[h, 0, :, :, h, 0] = cosines
+        table[h, 0, :, :, h, 1] = -sines
+        table[h, 1, :, :, h, 0] = -sines
+        table[h, 1, :, :, h, 1] = -cosines
+    return bf16(table.reshape(2, 2, NY, LANES))
 
 
 def x_analysis():
@@ -124,7 +123,7 @@
     return jnp.where(index(a.shape, 1) < HALF, pltpu.roll(a, HALF, 1), b)
 
 
-def analyse_kernel(f_hbm, g_hbm, y_hbm, x_hbm, out_ref, f_ref, g_ref, y_ref, x_ref, planes, sems):
+def analyse_kernel(f_hbm, g_hbm, y_hbm, x_hbm, out_ref, f_ref, g_ref, y_ref, x_ref, sums, planes, sems):
     copies = [
         pltpu.make_async_copy(y_hbm, y_ref, sems.at[0]),
         pltpu.make_async_copy(x_hbm, x_ref, sems.at[1]),
@@ -143,12 +142,19 @@
     for c in range(CHANS):
         copies[2 + 2 * c].wait()
         copies[3 + 2 * c].wait()
-        both = dot(f_ref[c].reshape(rows, NY), y_ref[0]) + dot(g_ref[c].reshape(rows, NY), y_ref[1])
-        both = both.astype(BF16)
-        for z in range(CELLS):
-            part = dot(x_ref[...], both[z * NX : (z + 1) * NX])
-            start = (c // 2 * ROWS + c % 2 * CELLS + z) * MX
-            planes[start : start + MX, :] = part[:MX, :LANES] + part[MX:, LANES:]
+        for h, v in enumerate((f_ref, g_ref)):
+            for z in range(CELLS):
+                part = dot(x_ref[...], v[c, z]).astype(BF16)
+                start = (c * CELLS + z) * MX
+                for r in range(2):
+                    sums[h, r, start : start + MX, :] = part[r * MX : (r + 1) * MX]
+    total = 0.0
+    for h in range(2):
+        for r in range(2):
+            total = total + dot(sums[h, r], y_ref[h, r])
+    for ch in range(2):
+        start = ch * ROWS * MX
+        planes[start : start + USED * MX, :] = total[ch * USED * MX : (ch + 1) * USED * MX]
     for p in range(MX):
         first = planes[pl.ds(p, ROWS, stride=MX), :]
         second = planes[pl.ds(ROWS * MX + p, ROWS, stride=MX), :]
@@ -156,15 +162,23 @@
         out_ref[N_SPACE + p] = high_halves(first, second).astype(BF16)
 
 
+def in_hbm(values):
+    return pltpu.with_memory_space_constraint(values, pltpu.HBM)
+
+
 def message():
     return jax.ShapeDtypeStruct((PAIR * N_SPACE, ROWS, LANES), BF16)
 
 
+def small_message():
+    return jax.ShapeDtypeStruct((2 * N_LINE, LANES), F32)
+
+
 def field_buffer():
     return pltpu.VMEM((CHANS, CELLS, NX, NY), BF16)
 
 
-def call(kernel, name, out_shape, *operands, in_specs=None, out_specs=None, scratch=(), vmem=VMEM_LIMIT):
+def call(kernel, name, out_shape, *operands, in_specs=None, out_specs=None, scratch=()):
     whole = pl.BlockSpec(memory_space=pltpu.VMEM)
     return pl.pallas_call(
         kernel,
@@ -172,7 +186,7 @@
         out_specs=out_specs or jax.tree.map(lambda _: whole, out_shape),
         out_shape=out_shape,
         scratch_shapes=list(scratch),
-        compiler_params=pltpu.CompilerParams(vmem_limit_bytes=vmem),
+        compiler_params=pltpu.CompilerParams(vmem_limit_bytes=VMEM_LIMIT),
         name=name,
     )(*operands)
 
@@ -182,20 +196,17 @@
         analyse_kernel,
         "analyse",
         message(),
-        field,
-        cotangent,
-        y_analysis(),
-        x_analysis(),
+        *(in_hbm(v) for v in (field, cotangent, y_analysis(), x_analysis())),
         in_specs=[pl.BlockSpec(memory_space=pltpu.HBM)] * 4,
         scratch=[
             field_buffer(),
             field_buffer(),
-            pltpu.VMEM((2, NY, 2 * LANES), BF16),
+            pltpu.VMEM((2, 2, NY, LANES), BF16),
             pltpu.VMEM((2 * MX, NX), BF16),
+            pltpu.VMEM((2, 2, 4 * CELLS * MX, NY), BF16),
             pltpu.VMEM((2 * ROWS * MX, LANES), F32),
             pltpu.SemaphoreType.DMA((2 + 2 * CHANS,)),
         ],
-        vmem=ALL_VMEM,
     )
 
 
@@ -241,18 +252,20 @@
     chan_ref[...] = spec.reshape(4 * MZ, LANES)
     fr, fi, gr, gi = (spec[i] for i in range(4))
     f = jnp.concatenate([fr, fi], 0).astype(BF16)
-    f_turned = jnp.concatenate([-fi, fr], 0).astype(BF16)
     g = jnp.concatenate([gr, gi], 0).astype(BF16)
-    g_turned = jnp.concatenate([gi, -gr], 0).astype(BF16)
-    own = index((2 * MZ, LANES), 0) % MZ
-    mixed = jnp.zeros((2 * MZ, LANES), F32)
-    grad = jnp.zeros((2 * MZ, LANES), F32)
+    own = index((2 * MZ, 2 * LANES), 0) % MZ
+    by_f = jnp.zeros((2 * MZ, 2 * LANES), F32)
+    by_g = jnp.zeros((2 * MZ, 2 * LANES), F32)
     for k in range(MZ):
-        w_real = w_ref[0, 0, k, 0]
-        w_imag = w_ref[0, 0, k, 1]
-        mixed = jnp.where(own == k, dot_last(f, w_real) + dot_last(f_turned, w_imag), mixed)
-        grad = jnp.where(own == k, dot(g, w_real) + dot(g_turned, w_imag), grad)
-    back = jnp.concatenate([mixed, grad], 0).reshape(4, 1, MZ, LANES)
+        both = w_ref[0, 0, k]
+        by_f = jnp.where(own == k, dot_last(f, both.reshape(2 * LANES, LANES)), by_f)
+        by_g = jnp.where(own == k, dot(g, jnp.concatenate([both[0], both[1]], 1)), by_g)
+    mixed_real = by_f[:MZ, :LANES] - by_f[MZ:, LANES:]
+    mixed_imag = by_f[MZ:, :LANES] + by_f[:MZ, LANES:]
+    grad_real = by_g[:MZ, :LANES] + by_g[MZ:, LANES:]
+    grad_imag = by_g[MZ:, :LANES] - by_g[:MZ, LANES:]
+    back = jnp.concatenate([mixed_real, mixed_imag, grad_real, grad_imag], 0)
+    back = back.reshape(4, 1, MZ, LANES)
     shape = (4, 4, MZ, LANES)
     spread = jnp.where(channel_part(shape) == index(shape, 1), back, 0.0).astype(BF16)
     back_ref[...] = dot_last(pick, spread.reshape(LANES, LANES))
@@ -276,43 +289,60 @@
     out_ref[...] = zback.reshape(PAIR * N_SPACE, ROWS, LANES)
 
 
-def synthesize_kernel(zback_ref, x_ref, y_ref, out_hbm, grad_hbm, out_ref, grad_ref, planes, sems):
+def synthesize_kernel(
+    zback_ref, chan_ref, x_ref, y_ref, out_hbm, grad_hbm, wgrad_hbm, out_ref, grad_ref, wgrad_ref, planes, mids, sems
+):
+    copies = []
+
+    def send(source, target):
+        copy = pltpu.make_async_copy(source, target, sems.at[len(copies)])
+        copy.start()
+        copies.append(copy)
+
     planes[...] = zback_ref[...].astype(F32).reshape(PAIR * N_SPACE * ROWS, LANES)
-    copies = []
+    columns = chan_ref[2 * MZ :, :].T
+    for k in range(MZ):
+        fr, fi = (chan_ref[i * MZ + k : i * MZ + k + 1, :] for i in range(2))
+        gr, gi = (columns[:, i * MZ + k : i * MZ + k + 1] for i in range(2))
+        wgrad_ref[k, 0] = gr * fr + gi * fi
+        wgrad_ref[k, 1] = gi * fr - gr * fi
+    send(wgrad_ref, wgrad_hbm.at[0, 0])
     for c in range(CHANS):
-        parts = []
         for z in range(CELLS):
             row = c % 2 * CELLS + z
             first = planes[pl.ds(row, MX, stride=ROWS), :]
             second = planes[pl.ds(MX * ROWS + row, MX, stride=ROWS), :]
             plane = low_halves(first, second) if c < 2 else high_halves(first, second)
             stacked = jnp.concatenate([plane, times_i(plane)], 0).astype(BF16)
-            parts.append(dot(x_ref[...], stacked).astype(BF16))
-        both = jnp.concatenate(parts, 0)
+            mids[c, z * NX : (z + 1) * NX, :] = dot(x_ref[...], stacked).astype(BF16)
+    for c in range(CHANS):
+        both = mids[c]
         for i, (buffer, target) in enumerate(((out_ref, out_hbm), (grad_ref, grad_hbm))):
             buffer[c] = dot(both, y_ref[i]).astype(BF16).reshape(CELLS, NX, NY)
-            copy = pltpu.make_async_copy(buffer.at[c], target.at[c], sems.at[2 * c + i])
-            copy.start()
-            copies.append(copy)
+            send(buffer.at[c], target.at[c])
     for copy in copies:
         copy.wait()
 
 
-def synthesize(zback):
+def synthesize(zback, chan):
     shape = jax.ShapeDtypeStruct((CHANS, CELLS, NX, NY), BF16)
+    wgrad = (MZ, 2, LANES, LANES)
     return call(
         synthesize_kernel,
         "synthesize",
-        (shape, shape),
+        (shape, shape, jax.ShapeDtypeStruct((1, 1) + wgrad, F32)),
         zback,
+        chan,
         x_synthesis(),
         y_synthesis(),
-        out_specs=(pl.BlockSpec(memory_space=pltpu.HBM),) * 2,
+        out_specs=(pl.BlockSpec(memory_space=pltpu.HBM),) * 3,
         scratch=[
             field_buffer(),
             field_buffer(),
+            pltpu.VMEM(wgrad, F32),
             pltpu.VMEM((PAIR * N_SPACE * ROWS, LANES), F32),
-            pltpu.SemaphoreType.DMA((2 * CHANS,)),
+            pltpu.VMEM((CHANS, CELLS * NX, LANES), BF16),
+            pltpu.SemaphoreType.DMA((2 * CHANS + 1,)),
         ],
     )
 
@@ -332,19 +362,25 @@
     return values.reshape(2 * N_LINE, LANES)
 
 
+def sum_z(planes):
+    return call(sum_z_kernel, "sum_z", small_message(), planes, bf16(z_table()))
+
+
+def mix(spec, weights):
+    return call(mix_kernel, "mix", (small_message(), small_message()), spec, weights)
+
+
+def spread_z(back):
+    return call(spread_z_kernel, "spread_z", message(), back, bf16(z_table().T))
+
+
 def shards(input_field, cotangent, weights):
     planes = outer(analyse(input_field, cotangent))
-    small = jax.ShapeDtypeStruct((2 * N_LINE, LANES), F32)
-    table = z_table()
-    spec = inner(call(sum_z_kernel, "sum_z", small, planes, bf16(table)))
-    back, chan = call(mix_kernel, "mix", (small, small), spec, weights)
+    spec = inner(sum_z(planes))
+    back, chan = mix(spec, weights)
     back = inner(back)
-    fr, fi, gr, gi = (chan[i * MZ : (i + 1) * MZ] for i in range(4))
-    go, fc = (lambda v: v[:, :, None]), (lambda v: v[:, None, :])
-    weight_grad = jnp.stack([go(gr) * fc(fr) + go(gi) * fc(fi), go(gi) * fc(fr) - go(gr) * fc(fi)], 1)[None, None]
-    zback = outer(call(spread_z_kernel, "spread_z", message(), back, bf16(table.T)))
-    spectral_out, field_grad = synthesize(zback)
-    return (spectral_out, field_grad, weight_grad)
+    zback = outer(spread_z(back))
+    return synthesize(zback, chan)
 
 
 def solution(mesh):

time: 74.3 us -> 69.5 us (0.935)
  blocking collectives: 39.4 us -> 61.8 us
  waiting for transfers between devices: 15.2 us -> 0 us
  starting transfers between devices: 7.54 us -> 0 us
  Pallas kernels: 9.65 us -> 6.7 us
  other arithmetic: 1.41 us -> 0 us
    all_to_all x2 -> x0, waiting for transfers between devices: 15.2 us -> none  [the longest x1 7.78 us: outer(): lax.all_to_all(values, ('blk', 'space'), 0, 0, tiled=True, axis_index_gro...]
    all_to_all x1 -> x2, blocking collectives: 23 us -> 35.2 us  [outer(): lax.all_to_all(values, ('blk', 'space'), 0, 0, tiled=True, axis_index_gro...]
    all_to_all x1 -> x2, blocking collectives: 16.4 us -> 26.6 us  [inner(): lax.all_to_all(values, 'blk', 0, 0, tiled=True, axis_index_groups=groups)]
    all_to_all x2 -> x0, starting transfers between devices: 7.54 us -> none  [the longest x1 3.86 us: outer(): lax.all_to_all(values, ('blk', 'space'), 0, 0, tiled=True, axis_index_gro...]
    pallas_call x5, Pallas kernels: 9.65 us -> 6.7 us  [call(): pl.pallas_call(kernel, in_specs=in_specs or [whole] * len(operands), out_...]
    broadcast_in_dim x1 -> x0, other arithmetic: 1.07 us -> none  [shards(): jnp.stack([go(gr) * fc(fr) + go(gi) * fc(fi), go(gi) * fc(fr) - go(gr) *...]
  transfers between devices with their start and end apart: 2 -> 0, of which waited for: 2 -> 0; matrix products, arithmetic and copies ran while one was open for 2% -> 0% of each run, Pallas kernels for 0% -> 0%
where the time goes in v3:
time: 69.5 us; the launch traced here: 69.2 us
  blocking collectives  61.8 us (89%)
  Pallas kernels  6.7 us (10%)
    all_to_all x2, blocking collectives, outer(): lax.all_to_all(values, ('blk', 'space'), 0, 0, tiled=True, axis_index_gro...  35.2 us
    all_to_all x2, blocking collectives, inner(): lax.all_to_all(values, 'blk', 0, 0, tiled=True, axis_index_groups=groups)  26.6 us
    pallas_call x5, Pallas kernels, call(): pl.pallas_call(kernel, in_specs=in_specs or [whole] * len(operands), out_...  6.7 us

profile of v3, /device:TPU:1, one launch (start us, length us, event | category | flops | bytes accessed | tf_op | source)
XLA Modules:
  0.0 69.2 jit_solution(10376030199767101904)
XLA Ops:
  0.6 0.0 copy-start.3
  0.6 0.0 copy-start
  0.7 2.6 %analyse.1 = bf16[32,16,128]{2,1,0:T(8,128)(2,1)S(1)} custom-call(bf16[4,6,96,192]{3,2,1,0:T(8,128)(2,1)} %f_hbm.1, bf16[4,6,96,192]{3,2,1,0:T(8,128)(2,1)} %g_hbm.1, bf16[2,2,192,128]{3,2,1,0:T(8,128)(2,1)} %constant.12.clone.y_hbm, bf16[32,96]{1,0:T(8,128)(2,1)} %constant.13.clone.x_hbm), custom_call_target="tpu_custom_call" | custom-call | tf_op jit(solution)/shard_map/analyse/pallas_call | solution.py:183
  3.2 0.0 copy-start.2
  3.2 0.0 copy-start.1
  3.3 0.0 copy-start.4
  3.3 22.8 %all_to_all.20.planes_ref = bf16[32,16,128]{2,1,0:T(8,128)(2,1)S(1)} all-to-all(bf16[32,16,128]{2,1,0:T(8,128)(2,1)S(1)} %analyse.1), channel_id=1, replica_groups={{0,1,2,3,4,5,6,7,8,9,10,11,12,13,14,15,256,257,258,259,260,261,262,263,..., dimensions={0} | all-to-all | bytes 262144 | tf_op jit(solution)/shard_map/all_to_all | solution.py:355
  26.1 0.0 copy-done.3
  26.1 0.4 sum_z.1
  26.5 16.4 %all_to_all.21 = f32[16,2,128]{2,1,0:T(2,128)S(1)} all-to-all(f32[16,2,128]{2,1,0:T(2,128)S(1)} %bitcast.6), channel_id=1, replica_groups={{0,16,32,48,64,80,96,112,128,144,160,176,192,208,224,240},{256,272,288,..., dimensions={0} | all-to-all | bytes 32768 | tf_op jit(solution)/shard_map/all_to_all | solution.py:361
  42.8 0.0 copy-done
  42.8 0.6 mix.1
  43.5 10.2 %all_to_all.22 = f32[16,2,128]{2,1,0:T(2,128)S(1)} all-to-all(f32[16,2,128]{2,1,0:T(2,128)S(1)} %bitcast.7), channel_id=1, replica_groups={{0,16,32,48,64,80,96,112,128,144,160,176,192,208,224,240},{256,272,288,..., dimensions={0} | all-to-all | bytes 32768 | tf_op jit(solution)/shard_map/all_to_all | solution.py:361
  53.7 0.0 copy-done.2
  53.7 0.4 spread_z.1
  54.1 12.4 %all_to_all.23.zback_ref = bf16[32,16,128]{2,1,0:T(8,128)(2,1)S(1)} all-to-all(bf16[32,16,128]{2,1,0:T(8,128)(2,1)S(1)} %spread_z.1), channel_id=1, replica_groups={{0,1,2,3,4,5,6,7,8,9,10,11,12,13,14,15,256,257,258,259,260,261,262,263,..., dimensions={0} | all-to-all | bytes 262144 | tf_op jit(solution)/shard_map/all_to_all | solution.py:355
  66.5 0.0 copy-done.1
  66.5 0.0 copy-done.4
  66.5 2.7 %synthesize.1 = (bf16[4,6,96,192]{3,2,1,0:T(8,128)(2,1)}, bf16[4,6,96,192]{3,2,1,0:T(8,128)(2,1)}, f32[1,1,8,2,128,128]{5,4,3,2,1,0:T(8,128)}) custom-call(bf16[32,16,128]{2,1,0:T(8,128)(2,1)S(1)} %all_to_all.23.zback_ref, f32[32,128]{1,0:T(8,128)S(1)} %get-tuple-element.6.chan_ref, bf16[96,32]{1,0:T(8,128)(2,1)S(1)} %copy-done.4, ...), custom_call_target="tpu_custom_call" | custom-call | tf_op jit(solution)/shard_map/synthesize/pallas_call | solution.py:183
Async XLA Ops:
  0.6 25.5 %copy-start.3 = (bf16[64,512]{1,0:T(8,128)(2,1)S(1)}, bf16[64,512]{1,0:T(8,128)(2,1)}, u32[]{:S(2)}) copy-start(bf16[64,512]{1,0:T(8,128)(2,1)} %constant.14.clone.z_ref) | copy-start | bytes 196612
  0.6 42.2 %copy-start = (bf16[1,1,8,2,128,128]{5,4,3,2,1,0:T(8,128)(2,1)S(1)}, bf16[1,1,8,2,128,128]{5,4,3,2,1,0:T(8,128)(2,1)}, u32[]{:S(2)}) copy-start(bf16[1,1,8,2,128,128]{5,4,3,2,1,0:T(8,128)(2,1)} %w_ref.1) | copy-start | bytes 1572868
  3.2 50.5 %copy-start.2 = (bf16[512,64]{1,0:T(8,128)(2,1)S(1)}, bf16[512,64]{1,0:T(8,128)(2,1)}, u32[]{:S(2)}) copy-start(bf16[512,64]{1,0:T(8,128)(2,1)} %constant.15.clone.z_ref) | copy-start | bytes 196612
  3.2 63.3 %copy-start.1 = (bf16[2,128,192]{2,1,0:T(8,128)(2,1)S(1)}, bf16[2,128,192]{2,1,0:T(8,128)(2,1)}, u32[]{:S(2)}) copy-start(bf16[2,128,192]{2,1,0:T(8,128)(2,1)} %constant.17.clone.y_ref) | copy-start | bytes 294916
  3.3 63.2 %copy-start.4 = (bf16[96,32]{1,0:T(8,128)(2,1)S(1)}, bf16[96,32]{1,0:T(8,128)(2,1)}, u32[]{:S(2)}) copy-start(bf16[96,32]{1,0:T(8,128)(2,1)} %constant.16.clone.x_ref) | copy-start | bytes 18436

commit v4 on v3

--- a/solution.py
+++ b/solution.py
@@ -29,8 +29,17 @@
 FORWARD = 1.0 / math.sqrt(NX * NY * NZ)
 SYNTH = 1.0 / math.sqrt(MX * MY * MZ)
 VMEM_LIMIT = 48 * 1024 * 1024
+LEAD_X = 2
+LEAD_Z = 5
+LEAD_LINE = 9
 F32 = jnp.float32
 BF16 = jnp.bfloat16
+
+
+OUTER = [
+    ((LEAD_Z + z) % 8 % 2, (LEAD_X + x) % 4 * 4 + (LEAD_Z + z) % 8 // 2) for x in range(4) for z in range(8)
+]
+PLACE = {member: place for place, member in enumerate(OUTER)}
 
 
 def freqs(count):
@@ -72,6 +81,7 @@
             cells = slice(cl * CELLS, (cl + 1) * CELLS)
             table[0, pair, cl, :, pair, :, cells] = cosines
             table[1, pair, cl, :, pair, :, cells] = sines
+    table = table.reshape(2 * MODES, PAIR * N_SPACE, ROWS)[:, [pair * N_SPACE + space for pair, space in OUTER]]
     return table.reshape(2 * MODES, PAIR * N_SPACE * ROWS)
 
 
@@ -158,8 +168,8 @@
     for p in range(MX):
         first = planes[pl.ds(p, ROWS, stride=MX), :]
         second = planes[pl.ds(ROWS * MX + p, ROWS, stride=MX), :]
-        out_ref[p] = low_halves(first, second).astype(BF16)
-        out_ref[N_SPACE + p] = high_halves(first, second).astype(BF16)
+        out_ref[PLACE[0, p]] = low_halves(first, second).astype(BF16)
+        out_ref[PLACE[1, p]] = high_halves(first, second).astype(BF16)
 
 
 def in_hbm(values):
@@ -210,16 +220,20 @@
     )
 
 
+def line_place(line):
+    return (line + N_LINE - LEAD_LINE) % N_LINE
+
+
 def mode_picker(ch):
     shape = (2 * QS, LANES)
     row, lane = index(shape, 0), index(shape, 1)
-    return jnp.where(row == lane % QS * 2 + ch, 1.0, 0.0).astype(BF16)
+    return jnp.where(row == line_place(lane % QS) * 2 + ch, 1.0, 0.0).astype(BF16)
 
 
 def channel_picker():
     shape = (2 * N_LINE, LANES)
     row, lane = index(shape, 0), index(shape, 1)
-    return jnp.where(row == lane // 4 % N_LINE * 2 + lane // 2 % 2, 1.0, 0.0).astype(BF16)
+    return jnp.where(row == line_place(lane // 4 % N_LINE) * 2 + lane // 2 % 2, 1.0, 0.0).astype(BF16)
 
 
 def channel_part(shape):
@@ -299,7 +313,9 @@
         copy.start()
         copies.append(copy)
 
-    planes[...] = zback_ref[...].astype(F32).reshape(PAIR * N_SPACE * ROWS, LANES)
+    for place, (pair, space) in enumerate(OUTER):
+        start = (pair * N_SPACE + space) * ROWS
+        planes[start : start + ROWS, :] = zback_ref[place].astype(F32)
     columns = chan_ref[2 * MZ :, :].T
     for k in range(MZ):
         fr, fi = (chan_ref[i * MZ + k : i * MZ + k + 1, :] for i in range(2))
@@ -348,15 +364,13 @@
 
 
 def outer(values):
-    groups = [
-        [(pair * N_LINE + line) * N_SPACE + s for pair in range(PAIR) for s in range(N_SPACE)]
-        for line in range(N_LINE)
-    ]
+    groups = [[(pair * N_LINE + line) * N_SPACE + space for pair, space in OUTER] for line in range(N_LINE)]
     return lax.all_to_all(values, ("blk", "space"), 0, 0, tiled=True, axis_index_groups=groups)
 
 
 def inner(values):
-    groups = [[pair * N_LINE + line for line in range(N_LINE)] for pair in range(PAIR)]
+    lines = [(LEAD_LINE + place) % N_LINE for place in range(N_LINE)]
+    groups = [[pair * N_LINE + line for line in lines] for pair in range(PAIR)]
     values = values.reshape(N_LINE, 2, LANES)
     values = lax.all_to_all(values, "blk", 0, 0, tiled=True, axis_index_groups=groups)
     return values.reshape(2 * N_LINE, LANES)

time: 69.5 us -> 62.1 us (0.89)
  blocking collectives: 61.8 us -> 54.4 us
    all_to_all x2, blocking collectives: 26.6 us -> 21.2 us  [inner(): lax.all_to_all(values, 'blk', 0, 0, tiled=True, axis_index_groups=groups)]
    all_to_all x2, blocking collectives: 35.2 us -> 33.2 us  [outer(): lax.all_to_all(values, ('blk', 'space'), 0, 0, tiled=True, axis_index_gro...]
where the time goes in v4:
time: 62.1 us; the launch traced here: 61.9 us
  blocking collectives  54.4 us (88%)
  Pallas kernels  6.71 us (11%)
  between operations  0.69 us (1%)
    all_to_all x2, blocking collectives, outer(): lax.all_to_all(values, ('blk', 'space'), 0, 0, tiled=True, axis_index_gro...  33.2 us
    all_to_all x2, blocking collectives, inner(): lax.all_to_all(values, 'blk', 0, 0, tiled=True, axis_index_groups=groups)  21.2 us
    pallas_call x5, Pallas kernels, call(): pl.pallas_call(kernel, in_specs=in_specs or [whole] * len(operands), out_...  6.71 us

profile of v4, /device:TPU:1, one launch (start us, length us, event | category | flops | bytes accessed | tf_op | source)
XLA Modules:
  0.0 61.9 jit_solution(628416170591413379)
XLA Ops:
  0.6 0.0 copy-start.3
  0.6 0.0 copy-start
  0.7 2.6 %analyse.1 = bf16[32,16,128]{2,1,0:T(8,128)(2,1)S(1)} custom-call(bf16[4,6,96,192]{3,2,1,0:T(8,128)(2,1)} %f_hbm.1, bf16[4,6,96,192]{3,2,1,0:T(8,128)(2,1)} %g_hbm.1, bf16[2,2,192,128]{3,2,1,0:T(8,128)(2,1)} %constant.12.clone.y_hbm, bf16[32,96]{1,0:T(8,128)(2,1)} %constant.13.clone.x_hbm), custom_call_target="tpu_custom_call" | custom-call | tf_op jit(solution)/shard_map/analyse/pallas_call | solution.py:193
  3.2 0.0 copy-start.2
  3.2 0.0 copy-start.1
  3.3 0.0 copy-start.4
  3.3 20.0 %all_to_all.20.planes_ref = bf16[32,16,128]{2,1,0:T(8,128)(2,1)S(1)} all-to-all(bf16[32,16,128]{2,1,0:T(8,128)(2,1)S(1)} %analyse.1), channel_id=1, replica_groups={{266,11,267,8,264,9,265,10,270,15,271,12,268,13,269,14,258,3,259,0,256,..., dimensions={0} | all-to-all | bytes 262144 | tf_op jit(solution)/shard_map/all_to_all | solution.py:368
  23.3 0.0 copy-done.3
  23.3 0.4 sum_z.1
  23.6 11.4 %all_to_all.21 = f32[16,2,128]{2,1,0:T(2,128)S(1)} all-to-all(f32[16,2,128]{2,1,0:T(2,128)S(1)} %bitcast.6), channel_id=1, replica_groups={{144,160,176,192,208,224,240,0,16,32,48,64,80,96,112,128},{400,416,432,..., dimensions={0} | all-to-all | bytes 32768 | tf_op jit(solution)/shard_map/all_to_all | solution.py:375
  35.0 0.0 copy-done
  35.0 0.6 %mix.1 = (f32[32,128]{1,0:T(8,128)S(1)}, f32[32,128]{1,0:T(8,128)S(1)}) custom-call(f32[32,128]{1,0:T(8,128)S(1)} %bitcast.4, bf16[1,1,8,2,128,128]{5,4,3,2,1,0:T(8,128)(2,1)S(1)} %copy-done), custom_call_target="tpu_custom_call" | custom-call | tf_op jit(solution)/shard_map/mix/pallas_call | solution.py:193
  35.7 9.9 %all_to_all.22 = f32[16,2,128]{2,1,0:T(2,128)S(1)} all-to-all(f32[16,2,128]{2,1,0:T(2,128)S(1)} %bitcast.7), channel_id=1, replica_groups={{144,160,176,192,208,224,240,0,16,32,48,64,80,96,112,128},{400,416,432,..., dimensions={0} | all-to-all | bytes 32768 | tf_op jit(solution)/shard_map/all_to_all | solution.py:375
  45.5 0.0 copy-done.2
  45.5 0.4 spread_z.1
  46.0 13.2 %all_to_all.23.zback_ref = bf16[32,16,128]{2,1,0:T(8,128)(2,1)S(1)} all-to-all(bf16[32,16,128]{2,1,0:T(8,128)(2,1)S(1)} %spread_z.1), channel_id=1, replica_groups={{266,11,267,8,264,9,265,10,270,15,271,12,268,13,269,14,258,3,259,0,256,..., dimensions={0} | all-to-all | bytes 262144 | tf_op jit(solution)/shard_map/all_to_all | solution.py:368
  59.1 0.0 copy-done.1
  59.1 0.0 copy-done.4
  59.1 2.7 %synthesize.1 = (bf16[4,6,96,192]{3,2,1,0:T(8,128)(2,1)}, bf16[4,6,96,192]{3,2,1,0:T(8,128)(2,1)}, f32[1,1,8,2,128,128]{5,4,3,2,1,0:T(8,128)}) custom-call(bf16[32,16,128]{2,1,0:T(8,128)(2,1)S(1)} %all_to_all.23.zback_ref, f32[32,128]{1,0:T(8,128)S(1)} %get-tuple-element.6.chan_ref, bf16[96,32]{1,0:T(8,128)(2,1)S(1)} %copy-done.4, ...), custom_call_target="tpu_custom_call" | custom-call | tf_op jit(solution)/shard_map/synthesize/pallas_call | solution.py:193
Async XLA Ops:
  0.6 22.6 %copy-start.3 = (bf16[64,512]{1,0:T(8,128)(2,1)S(1)}, bf16[64,512]{1,0:T(8,128)(2,1)}, u32[]{:S(2)}) copy-start(bf16[64,512]{1,0:T(8,128)(2,1)} %constant.14.clone.z_ref) | copy-start | bytes 196612
  0.6 34.4 %copy-start = (bf16[1,1,8,2,128,128]{5,4,3,2,1,0:T(8,128)(2,1)S(1)}, bf16[1,1,8,2,128,128]{5,4,3,2,1,0:T(8,128)(2,1)}, u32[]{:S(2)}) copy-start(bf16[1,1,8,2,128,128]{5,4,3,2,1,0:T(8,128)(2,1)} %w_ref.1) | copy-start | bytes 1572868
  3.2 42.3 %copy-start.2 = (bf16[512,64]{1,0:T(8,128)(2,1)S(1)}, bf16[512,64]{1,0:T(8,128)(2,1)}, u32[]{:S(2)}) copy-start(bf16[512,64]{1,0:T(8,128)(2,1)} %constant.15.clone.z_ref) | copy-start | bytes 196612
  3.2 55.9 %copy-start.1 = (bf16[2,128,192]{2,1,0:T(8,128)(2,1)S(1)}, bf16[2,128,192]{2,1,0:T(8,128)(2,1)}, u32[]{:S(2)}) copy-start(bf16[2,128,192]{2,1,0:T(8,128)(2,1)} %constant.17.clone.y_ref) | copy-start | bytes 294916
  3.3 55.9 %copy-start.4 = (bf16[96,32]{1,0:T(8,128)(2,1)S(1)}, bf16[96,32]{1,0:T(8,128)(2,1)}, u32[]{:S(2)}) copy-start(bf16[96,32]{1,0:T(8,128)(2,1)} %constant.16.clone.x_ref) | copy-start | bytes 18436

commit v5 on v4

--- a/solution.py
+++ b/solution.py
@@ -134,37 +134,35 @@
 
 
 def analyse_kernel(f_hbm, g_hbm, y_hbm, x_hbm, out_ref, f_ref, g_ref, y_ref, x_ref, sums, planes, sems):
-    copies = [
-        pltpu.make_async_copy(y_hbm, y_ref, sems.at[0]),
-        pltpu.make_async_copy(x_hbm, x_ref, sems.at[1]),
-    ]
+    copies = [pltpu.make_async_copy(x_hbm, x_ref, sems.at[1])]
     for c in range(CHANS):
         copies.append(pltpu.make_async_copy(f_hbm.at[c], f_ref.at[c], sems.at[2 + 2 * c]))
         copies.append(pltpu.make_async_copy(g_hbm.at[c], g_ref.at[c], sems.at[3 + 2 * c]))
+    copies.append(pltpu.make_async_copy(y_hbm, y_ref, sems.at[0]))
     for copy in copies:
         copy.start()
     for ch in range(2):
         start = (ch * ROWS + USED) * MX
         planes[start : start + (ROWS - USED) * MX, :] = jnp.zeros(((ROWS - USED) * MX, LANES), F32)
-    rows = CELLS * NX
     copies[0].wait()
-    copies[1].wait()
     for c in range(CHANS):
+        copies[1 + 2 * c].wait()
         copies[2 + 2 * c].wait()
-        copies[3 + 2 * c].wait()
         for h, v in enumerate((f_ref, g_ref)):
             for z in range(CELLS):
                 part = dot(x_ref[...], v[c, z]).astype(BF16)
                 start = (c * CELLS + z) * MX
                 for r in range(2):
                     sums[h, r, start : start + MX, :] = part[r * MX : (r + 1) * MX]
-    total = 0.0
-    for h in range(2):
-        for r in range(2):
-            total = total + dot(sums[h, r], y_ref[h, r])
+    copies[-1].wait()
     for ch in range(2):
+        half = slice(ch * USED * MX, (ch + 1) * USED * MX)
+        total = 0.0
+        for h in range(2):
+            for r in range(2):
+                total = total + dot(sums[h, r, half], y_ref[h, r])
         start = ch * ROWS * MX
-        planes[start : start + USED * MX, :] = total[ch * USED * MX : (ch + 1) * USED * MX]
+        planes[start : start + USED * MX, :] = total
     for p in range(MX):
         first = planes[pl.ds(p, ROWS, stride=MX), :]
         second = planes[pl.ds(ROWS * MX + p, ROWS, stride=MX), :]
@@ -316,26 +314,42 @@
     for place, (pair, space) in enumerate(OUTER):
         start = (pair * N_SPACE + space) * ROWS
         planes[start : start + ROWS, :] = zback_ref[place].astype(F32)
-    columns = chan_ref[2 * MZ :, :].T
+    columns = chan_ref[2 * MZ :, :].T.astype(BF16)
+    fr, fi = chan_ref[:MZ, :], chan_ref[MZ : 2 * MZ, :]
+    pairs = jnp.concatenate([jnp.concatenate([fr, -fi], 1), jnp.concatenate([fi, fr], 1)], 0)
+    own = index(pairs.shape, 0) % MZ
+
     for k in range(MZ):
-        fr, fi = (chan_ref[i * MZ + k : i * MZ + k + 1, :] for i in range(2))
-        gr, gi = (columns[:, i * MZ + k : i * MZ + k + 1] for i in range(2))
-        wgrad_ref[k, 0] = gr * fr + gi * fi
-        wgrad_ref[k, 1] = gi * fr - gr * fi
+        both = dot(columns, jnp.where(own == k, pairs, 0.0).astype(BF16))
+        wgrad_ref[k, 0] = both[:, :LANES]
+        wgrad_ref[k, 1] = both[:, LANES:]
     send(wgrad_ref, wgrad_hbm.at[0, 0])
-    for c in range(CHANS):
-        for z in range(CELLS):
-            row = c % 2 * CELLS + z
-            first = planes[pl.ds(row, MX, stride=ROWS), :]
-            second = planes[pl.ds(MX * ROWS + row, MX, stride=ROWS), :]
-            plane = low_halves(first, second) if c < 2 else high_halves(first, second)
-            stacked = jnp.concatenate([plane, times_i(plane)], 0).astype(BF16)
-            mids[c, z * NX : (z + 1) * NX, :] = dot(x_ref[...], stacked).astype(BF16)
-    for c in range(CHANS):
+
+    def turned(c, z):
+        row = c % 2 * CELLS + z
+        first = planes[pl.ds(row, MX, stride=ROWS), :]
+        second = planes[pl.ds(MX * ROWS + row, MX, stride=ROWS), :]
+        plane = low_halves(first, second) if c < 2 else high_halves(first, second)
+        return jnp.concatenate([plane, times_i(plane)], 0).astype(BF16)
+
+    def x_part(c):
+        for z in range(0, CELLS, 2):
+            stacked = jnp.concatenate([turned(c, z), turned(c, z + 1)], 1)
+            both = dot(x_ref[...], stacked).astype(BF16)
+            mids[c, z * NX : (z + 1) * NX, :] = both[:, :LANES]
+            mids[c, (z + 1) * NX : (z + 2) * NX, :] = both[:, LANES:]
+
+    def y_part(c):
         both = mids[c]
         for i, (buffer, target) in enumerate(((out_ref, out_hbm), (grad_ref, grad_hbm))):
             buffer[c] = dot(both, y_ref[i]).astype(BF16).reshape(CELLS, NX, NY)
             send(buffer.at[c], target.at[c])
+
+    x_part(0)
+    for c in range(CHANS):
+        if c + 1 < CHANS:
+            x_part(c + 1)
+        y_part(c)
     for copy in copies:
         copy.wait()
 

time: 62.1 us -> 61.6 us (level)
  no operation moved by 1% of the time
where the time goes in v5:
time: 61.6 us; the launch traced here: 61.4 us
  blocking collectives  54.4 us (88%)
  Pallas kernels  6.22 us (10%)
  between operations  0.69 us (1%)
    all_to_all x2, blocking collectives, outer(): lax.all_to_all(values, ('blk', 'space'), 0, 0, tiled=True, axis_index_gro...  33.2 us
    all_to_all x2, blocking collectives, inner(): lax.all_to_all(values, 'blk', 0, 0, tiled=True, axis_index_groups=groups)  21.2 us
    pallas_call x5, Pallas kernels, call(): pl.pallas_call(kernel, in_specs=in_specs or [whole] * len(operands), out_...  6.22 us

profile of v5, /device:TPU:1, one launch (start us, length us, event | category | flops | bytes accessed | tf_op | source)
XLA Modules:
  0.0 61.4 jit_solution(16353188067648406696)
XLA Ops:
  0.6 0.0 copy-start.3
  0.6 0.0 copy-start
  0.7 2.6 %analyse.1 = bf16[32,16,128]{2,1,0:T(8,128)(2,1)S(1)} custom-call(bf16[4,6,96,192]{3,2,1,0:T(8,128)(2,1)} %f_hbm.1, bf16[4,6,96,192]{3,2,1,0:T(8,128)(2,1)} %g_hbm.1, bf16[2,2,192,128]{3,2,1,0:T(8,128)(2,1)} %constant.12.clone.y_hbm, bf16[32,96]{1,0:T(8,128)(2,1)} %constant.13.clone.x_hbm), custom_call_target="tpu_custom_call" | custom-call | tf_op jit(solution)/shard_map/analyse/pallas_call | solution.py:191
  3.3 0.0 copy-start.2
  3.3 0.0 copy-start.1
  3.3 0.0 copy-start.4
  3.3 20.0 %all_to_all.20.planes_ref = bf16[32,16,128]{2,1,0:T(8,128)(2,1)S(1)} all-to-all(bf16[32,16,128]{2,1,0:T(8,128)(2,1)S(1)} %analyse.1), channel_id=1, replica_groups={{266,11,267,8,264,9,265,10,270,15,271,12,268,13,269,14,258,3,259,0,256,..., dimensions={0} | all-to-all | bytes 262144 | tf_op jit(solution)/shard_map/all_to_all | solution.py:382
  23.3 0.0 copy-done.3
  23.3 0.4 sum_z.1
  23.7 11.4 %all_to_all.21 = f32[16,2,128]{2,1,0:T(2,128)S(1)} all-to-all(f32[16,2,128]{2,1,0:T(2,128)S(1)} %bitcast.6), channel_id=1, replica_groups={{144,160,176,192,208,224,240,0,16,32,48,64,80,96,112,128},{400,416,432,..., dimensions={0} | all-to-all | bytes 32768 | tf_op jit(solution)/shard_map/all_to_all | solution.py:389
  35.1 0.0 copy-done
  35.1 0.6 %mix.1 = (f32[32,128]{1,0:T(8,128)S(1)}, f32[32,128]{1,0:T(8,128)S(1)}) custom-call(f32[32,128]{1,0:T(8,128)S(1)} %bitcast.4, bf16[1,1,8,2,128,128]{5,4,3,2,1,0:T(8,128)(2,1)S(1)} %copy-done), custom_call_target="tpu_custom_call" | custom-call | tf_op jit(solution)/shard_map/mix/pallas_call | solution.py:191
  35.7 9.9 %all_to_all.22 = f32[16,2,128]{2,1,0:T(2,128)S(1)} all-to-all(f32[16,2,128]{2,1,0:T(2,128)S(1)} %bitcast.7), channel_id=1, replica_groups={{144,160,176,192,208,224,240,0,16,32,48,64,80,96,112,128},{400,416,432,..., dimensions={0} | all-to-all | bytes 32768 | tf_op jit(solution)/shard_map/all_to_all | solution.py:389
  45.6 0.0 copy-done.2
  45.6 0.4 spread_z.1
  46.0 13.2 %all_to_all.23.zback_ref = bf16[32,16,128]{2,1,0:T(8,128)(2,1)S(1)} all-to-all(bf16[32,16,128]{2,1,0:T(8,128)(2,1)S(1)} %spread_z.1), channel_id=1, replica_groups={{266,11,267,8,264,9,265,10,270,15,271,12,268,13,269,14,258,3,259,0,256,..., dimensions={0} | all-to-all | bytes 262144 | tf_op jit(solution)/shard_map/all_to_all | solution.py:382
  59.2 0.0 copy-done.1
  59.2 0.0 copy-done.4
  59.2 2.2 %synthesize.1 = (bf16[4,6,96,192]{3,2,1,0:T(8,128)(2,1)}, bf16[4,6,96,192]{3,2,1,0:T(8,128)(2,1)}, f32[1,1,8,2,128,128]{5,4,3,2,1,0:T(8,128)}) custom-call(bf16[32,16,128]{2,1,0:T(8,128)(2,1)S(1)} %all_to_all.23.zback_ref, f32[32,128]{1,0:T(8,128)S(1)} %get-tuple-element.6.chan_ref, bf16[96,32]{1,0:T(8,128)(2,1)S(1)} %copy-done.4, ...), custom_call_target="tpu_custom_call" | custom-call | tf_op jit(solution)/shard_map/synthesize/pallas_call | solution.py:191
Async XLA Ops:
  0.6 22.7 %copy-start.3 = (bf16[64,512]{1,0:T(8,128)(2,1)S(1)}, bf16[64,512]{1,0:T(8,128)(2,1)}, u32[]{:S(2)}) copy-start(bf16[64,512]{1,0:T(8,128)(2,1)} %constant.14.clone.z_ref) | copy-start | bytes 196612
  0.6 34.4 %copy-start = (bf16[1,1,8,2,128,128]{5,4,3,2,1,0:T(8,128)(2,1)S(1)}, bf16[1,1,8,2,128,128]{5,4,3,2,1,0:T(8,128)(2,1)}, u32[]{:S(2)}) copy-start(bf16[1,1,8,2,128,128]{5,4,3,2,1,0:T(8,128)(2,1)} %w_ref.1) | copy-start | bytes 1572868
  3.3 42.3 %copy-start.2 = (bf16[512,64]{1,0:T(8,128)(2,1)S(1)}, bf16[512,64]{1,0:T(8,128)(2,1)}, u32[]{:S(2)}) copy-start(bf16[512,64]{1,0:T(8,128)(2,1)} %constant.15.clone.z_ref) | copy-start | bytes 196612
  3.3 55.9 %copy-start.1 = (bf16[2,128,192]{2,1,0:T(8,128)(2,1)S(1)}, bf16[2,128,192]{2,1,0:T(8,128)(2,1)}, u32[]{:S(2)}) copy-start(bf16[2,128,192]{2,1,0:T(8,128)(2,1)} %constant.17.clone.y_ref) | copy-start | bytes 294916
  3.3 55.9 %copy-start.4 = (bf16[96,32]{1,0:T(8,128)(2,1)S(1)}, bf16[96,32]{1,0:T(8,128)(2,1)}, u32[]{:S(2)}) copy-start(bf16[96,32]{1,0:T(8,128)(2,1)} %constant.16.clone.x_ref) | copy-start | bytes 18436

commit v6 on v5

--- a/solution.py
+++ b/solution.py
@@ -29,17 +29,23 @@
 FORWARD = 1.0 / math.sqrt(NX * NY * NZ)
 SYNTH = 1.0 / math.sqrt(MX * MY * MZ)
 VMEM_LIMIT = 48 * 1024 * 1024
-LEAD_X = 2
-LEAD_Z = 5
-LEAD_LINE = 9
+FIRST_X = 2
+FIRST_Z = 5
+LAST_X = 2
+LAST_Z = 5
+THERE_LINE = 9
+BACK_LINE = 9
 F32 = jnp.float32
 BF16 = jnp.bfloat16
 
 
-OUTER = [
-    ((LEAD_Z + z) % 8 % 2, (LEAD_X + x) % 4 * 4 + (LEAD_Z + z) % 8 // 2) for x in range(4) for z in range(8)
-]
-PLACE = {member: place for place, member in enumerate(OUTER)}
+def members(lead_x, lead_z):
+    ring = [((lead_x + x) % 4, (lead_z + z) % 8) for x in range(4) for z in range(8)]
+    return [(z % 2, 4 * x + z // 2) for x, z in ring]
+
+
+FIRST = members(FIRST_X, FIRST_Z)
+LAST = members(LAST_X, LAST_Z)
 
 
 def freqs(count):
@@ -58,14 +64,13 @@
 
 
 def y_analysis():
-    cosines, sines = (v.T.reshape(NY, PAIR, QS) for v in phases(freqs(MY), NY))
-    table = np.zeros((2, 2, NY, PAIR, 2, 2, QS), np.float32)
-    for h in range(2):
-        table[h, 0, :, :, h, 0] = cosines
-        table[h, 0, :, :, h, 1] = -sines
-        table[h, 1, :, :, h, 0] = -sines
-        table[h, 1, :, :, h, 1] = -cosines
-    return bf16(table.reshape(2, 2, NY, LANES))
+    cosines, sines = (v.T.reshape(NY, PAIR, 1, QS) for v in phases(freqs(MY), NY))
+    table = np.zeros((2, NY, PAIR, 2, 2, QS), np.float32)
+    table[0, :, :, :, 0] = cosines
+    table[0, :, :, :, 1] = -sines
+    table[1, :, :, :, 0] = -sines
+    table[1, :, :, :, 1] = -cosines
+    return bf16(table.reshape(2, NY, LANES))
 
 
 def x_analysis():
@@ -73,7 +78,7 @@
     return bf16(np.concatenate([cosines, sines], 0))
 
 
-def z_table():
+def z_table(order):
     cosines, sines = (v.reshape(MZ, N_SPACE, CELLS) for v in phases(np.arange(MZ), NZ))
     table = np.zeros((2, PAIR, 2, MZ, PAIR, N_SPACE, ROWS), np.float32)
     for pair in range(PAIR):
@@ -81,7 +86,7 @@
             cells = slice(cl * CELLS, (cl + 1) * CELLS)
             table[0, pair, cl, :, pair, :, cells] = cosines
             table[1, pair, cl, :, pair, :, cells] = sines
-    table = table.reshape(2 * MODES, PAIR * N_SPACE, ROWS)[:, [pair * N_SPACE + space for pair, space in OUTER]]
+    table = table.reshape(2 * MODES, PAIR * N_SPACE, ROWS)[:, [pair * N_SPACE + space for pair, space in order]]
     return table.reshape(2 * MODES, PAIR * N_SPACE * ROWS)
 
 
@@ -148,26 +153,24 @@
     for c in range(CHANS):
         copies[1 + 2 * c].wait()
         copies[2 + 2 * c].wait()
-        for h, v in enumerate((f_ref, g_ref)):
-            for z in range(CELLS):
+        for z in range(CELLS):
+            for h, v in enumerate((f_ref, g_ref)):
                 part = dot(x_ref[...], v[c, z]).astype(BF16)
-                start = (c * CELLS + z) * MX
+                start = ((h * CHANS + c) * CELLS + z) * MX
                 for r in range(2):
-                    sums[h, r, start : start + MX, :] = part[r * MX : (r + 1) * MX]
+                    sums[r, start : start + MX, :] = part[r * MX : (r + 1) * MX]
     copies[-1].wait()
+    both = dot(sums[0], y_ref[0]) + dot(sums[1], y_ref[1])
+    half = 2 * USED * MX
+    total = jnp.where(index((half, LANES), 1) // (2 * QS) % 2 == 0, both[:half], both[half:])
     for ch in range(2):
-        half = slice(ch * USED * MX, (ch + 1) * USED * MX)
-        total = 0.0
-        for h in range(2):
-            for r in range(2):
-                total = total + dot(sums[h, r, half], y_ref[h, r])
         start = ch * ROWS * MX
-        planes[start : start + USED * MX, :] = total
+        planes[start : start + USED * MX, :] = total[ch * USED * MX : (ch + 1) * USED * MX]
     for p in range(MX):
         first = planes[pl.ds(p, ROWS, stride=MX), :]
         second = planes[pl.ds(ROWS * MX + p, ROWS, stride=MX), :]
-        out_ref[PLACE[0, p]] = low_halves(first, second).astype(BF16)
-        out_ref[PLACE[1, p]] = high_halves(first, second).astype(BF16)
+        out_ref[FIRST.index((0, p))] = low_halves(first, second).astype(BF16)
+        out_ref[FIRST.index((1, p))] = high_halves(first, second).astype(BF16)
 
 
 def in_hbm(values):
@@ -209,29 +212,29 @@
         scratch=[
             field_buffer(),
             field_buffer(),
-            pltpu.VMEM((2, 2, NY, LANES), BF16),
+            pltpu.VMEM((2, NY, LANES), BF16),
             pltpu.VMEM((2 * MX, NX), BF16),
-            pltpu.VMEM((2, 2, 4 * CELLS * MX, NY), BF16),
+            pltpu.VMEM((2, 2 * CHANS * CELLS * MX, NY), BF16),
             pltpu.VMEM((2 * ROWS * MX, LANES), F32),
             pltpu.SemaphoreType.DMA((2 + 2 * CHANS,)),
         ],
     )
 
 
-def line_place(line):
-    return (line + N_LINE - LEAD_LINE) % N_LINE
-
-
-def mode_picker(ch):
+def line_place(line, lead):
+    return (line + N_LINE - lead) % N_LINE
+
+
+def mode_picker(ch, lead):
     shape = (2 * QS, LANES)
     row, lane = index(shape, 0), index(shape, 1)
-    return jnp.where(row == line_place(lane % QS) * 2 + ch, 1.0, 0.0).astype(BF16)
-
-
-def channel_picker():
+    return jnp.where(row == line_place(lane % QS, lead) * 2 + ch, 1.0, 0.0).astype(BF16)
+
+
+def channel_picker(lead):
     shape = (2 * N_LINE, LANES)
     row, lane = index(shape, 0), index(shape, 1)
-    return jnp.where(row == line_place(lane // 4 % N_LINE) * 2 + lane // 2 % 2, 1.0, 0.0).astype(BF16)
+    return jnp.where(row == line_place(lane // 4 % N_LINE, lead) * 2 + lane // 2 % 2, 1.0, 0.0).astype(BF16)
 
 
 def channel_part(shape):
@@ -251,12 +254,11 @@
     spread = jnp.where(index(shape, 2) // QS == index(shape, 0), spec[None], 0.0).astype(BF16)
     spread = spread.reshape(8 * MODES, LANES)
     first, second = spread[:LANES], spread[LANES:]
-    out_ref[...] = dot_last(mode_picker(0), first) + dot_last(mode_picker(1), second)
+    out_ref[...] = dot_last(mode_picker(0, THERE_LINE), first) + dot_last(mode_picker(1, THERE_LINE), second)
 
 
 def mix_kernel(spec_ref, w_ref, back_ref, chan_ref):
-    pick = channel_picker()
-    wide = dot_first(spec_ref[...].astype(BF16), pick).reshape(4, 4, MZ, LANES)
+    wide = dot_first(spec_ref[...].astype(BF16), channel_picker(THERE_LINE)).reshape(4, 4, MZ, LANES)
     part = channel_part((4, MZ, LANES))
     spec = wide[:, 0]
     for j in range(1, 4):
@@ -280,7 +282,7 @@
     back = back.reshape(4, 1, MZ, LANES)
     shape = (4, 4, MZ, LANES)
     spread = jnp.where(channel_part(shape) == index(shape, 1), back, 0.0).astype(BF16)
-    back_ref[...] = dot_last(pick, spread.reshape(LANES, LANES))
+    back_ref[...] = dot_last(channel_picker(BACK_LINE), spread.reshape(LANES, LANES))
 
 
 def spread_z_kernel(back_ref, z_ref, out_ref):
@@ -288,7 +290,7 @@
     owner = index((MODES, LANES), 1) // QS
     spec = jnp.zeros((MODES, LANES), F32)
     for ch in range(2):
-        wide = dot_first(back, mode_picker(ch)).reshape(4, MODES, LANES)
+        wide = dot_first(back, mode_picker(ch, BACK_LINE)).reshape(4, MODES, LANES)
         for part in range(4):
             spec = jnp.where(owner == 4 * ch + part, wide[part], spec)
     field = owner // 2 % 2
@@ -311,7 +313,7 @@
         copy.start()
         copies.append(copy)
 
-    for place, (pair, space) in enumerate(OUTER):
+    for place, (pair, space) in enumerate(LAST):
         start = (pair * N_SPACE + space) * ROWS
         planes[start : start + ROWS, :] = zback_ref[place].astype(F32)
     columns = chan_ref[2 * MZ :, :].T.astype(BF16)
@@ -377,13 +379,13 @@
     )
 
 
-def outer(values):
-    groups = [[(pair * N_LINE + line) * N_SPACE + space for pair, space in OUTER] for line in range(N_LINE)]
+def outer(values, order):
+    groups = [[(pair * N_LINE + line) * N_SPACE + space for pair, space in order] for line in range(N_LINE)]
     return lax.all_to_all(values, ("blk", "space"), 0, 0, tiled=True, axis_index_groups=groups)
 
 
-def inner(values):
-    lines = [(LEAD_LINE + place) % N_LINE for place in range(N_LINE)]
+def inner(values, lead):
+    lines = [(lead + place) % N_LINE for place in range(N_LINE)]
     groups = [[pair * N_LINE + line for line in lines] for pair in range(PAIR)]
     values = values.reshape(N_LINE, 2, LANES)
     values = lax.all_to_all(values, "blk", 0, 0, tiled=True, axis_index_groups=groups)
@@ -391,7 +393,7 @@
 
 
 def sum_z(planes):
-    return call(sum_z_kernel, "sum_z", small_message(), planes, bf16(z_table()))
+    return call(sum_z_kernel, "sum_z", small_message(), planes, bf16(z_table(FIRST)))
 
 
 def mix(spec, weights):
@@ -399,15 +401,15 @@
 
 
 def spread_z(back):
-    return call(spread_z_kernel, "spread_z", message(), back, bf16(z_table().T))
+    return call(spread_z_kernel, "spread_z", message(), back, bf16(z_table(LAST).T))
 
 
 def shards(input_field, cotangent, weights):
-    planes = outer(analyse(input_field, cotangent))
-    spec = inner(sum_z(planes))
+    planes = outer(analyse(input_field, cotangent), FIRST)
+    spec = inner(sum_z(planes), THERE_LINE)
     back, chan = mix(spec, weights)
-    back = inner(back)
-    zback = outer(spread_z(back))
+    back = inner(back, BACK_LINE)
+    zback = outer(spread_z(back), LAST)
     return synthesize(zback, chan)
 
 

time: 61.6 us -> 61.6 us (level)
  no operation moved by 1% of the time
where the time goes in v6:
time: 61.6 us; the launch traced here: 61.4 us
  blocking collectives  54.4 us (88%)
  Pallas kernels  6.19 us (10%)
  between operations  0.69 us (1%)
    all_to_all x2, blocking collectives, outer(): lax.all_to_all(values, ('blk', 'space'), 0, 0, tiled=True, axis_index_gro...  33.2 us
    all_to_all x2, blocking collectives, inner(): lax.all_to_all(values, 'blk', 0, 0, tiled=True, axis_index_groups=groups)  21.2 us
    pallas_call x5, Pallas kernels, call(): pl.pallas_call(kernel, in_specs=in_specs or [whole] * len(operands), out_...  6.19 us

profile of v6, /device:TPU:1, one launch (start us, length us, event | category | flops | bytes accessed | tf_op | source)
XLA Modules:
  0.0 61.4 jit_solution(14299527654957474403)
XLA Ops:
  0.6 0.0 copy-start.3
  0.6 0.0 copy-start
  0.7 2.6 %analyse.1 = bf16[32,16,128]{2,1,0:T(8,128)(2,1)S(1)} custom-call(bf16[4,6,96,192]{3,2,1,0:T(8,128)(2,1)} %f_hbm.1, bf16[4,6,96,192]{3,2,1,0:T(8,128)(2,1)} %g_hbm.1, bf16[2,192,128]{2,1,0:T(8,128)(2,1)} %constant.12.clone.y_hbm, bf16[32,96]{1,0:T(8,128)(2,1)} %constant.13.clone.x_hbm), custom_call_target="tpu_custom_call" | custom-call | tf_op jit(solution)/shard_map/analyse/pallas_call | solution.py:194
  3.2 0.0 copy-start.2
  3.2 0.0 copy-start.1
  3.3 0.0 copy-start.4
  3.3 20.0 %all_to_all.20.planes_ref = bf16[32,16,128]{2,1,0:T(8,128)(2,1)S(1)} all-to-all(bf16[32,16,128]{2,1,0:T(8,128)(2,1)S(1)} %analyse.1), channel_id=1, replica_groups={{266,11,267,8,264,9,265,10,270,15,271,12,268,13,269,14,258,3,259,0,256,..., dimensions={0} | all-to-all | bytes 262144 | tf_op jit(solution)/shard_map/all_to_all | solution.py:384
  23.3 0.0 copy-done.3
  23.3 0.4 sum_z.1
  23.6 11.4 %all_to_all.21 = f32[16,2,128]{2,1,0:T(2,128)S(1)} all-to-all(f32[16,2,128]{2,1,0:T(2,128)S(1)} %bitcast.6), channel_id=1, replica_groups={{144,160,176,192,208,224,240,0,16,32,48,64,80,96,112,128},{400,416,432,..., dimensions={0} | all-to-all | bytes 32768 | tf_op jit(solution)/shard_map/all_to_all | solution.py:391
  35.0 0.0 copy-done
  35.0 0.6 %mix.1 = (f32[32,128]{1,0:T(8,128)S(1)}, f32[32,128]{1,0:T(8,128)S(1)}) custom-call(f32[32,128]{1,0:T(8,128)S(1)} %bitcast.4, bf16[1,1,8,2,128,128]{5,4,3,2,1,0:T(8,128)(2,1)S(1)} %copy-done), custom_call_target="tpu_custom_call" | custom-call | tf_op jit(solution)/shard_map/mix/pallas_call | solution.py:194
  35.7 9.9 %all_to_all.22 = f32[16,2,128]{2,1,0:T(2,128)S(1)} all-to-all(f32[16,2,128]{2,1,0:T(2,128)S(1)} %bitcast.7), channel_id=1, replica_groups={{144,160,176,192,208,224,240,0,16,32,48,64,80,96,112,128},{400,416,432,..., dimensions={0} | all-to-all | bytes 32768 | tf_op jit(solution)/shard_map/all_to_all | solution.py:391
  45.5 0.0 copy-done.2
  45.5 0.4 spread_z.1
  46.0 13.2 %all_to_all.23.zback_ref = bf16[32,16,128]{2,1,0:T(8,128)(2,1)S(1)} all-to-all(bf16[32,16,128]{2,1,0:T(8,128)(2,1)S(1)} %spread_z.1), channel_id=1, replica_groups={{266,11,267,8,264,9,265,10,270,15,271,12,268,13,269,14,258,3,259,0,256,..., dimensions={0} | all-to-all | bytes 262144 | tf_op jit(solution)/shard_map/all_to_all | solution.py:384
  59.1 0.0 copy-done.1
  59.2 0.0 copy-done.4
  59.2 2.2 %synthesize.1 = (bf16[4,6,96,192]{3,2,1,0:T(8,128)(2,1)}, bf16[4,6,96,192]{3,2,1,0:T(8,128)(2,1)}, f32[1,1,8,2,128,128]{5,4,3,2,1,0:T(8,128)}) custom-call(bf16[32,16,128]{2,1,0:T(8,128)(2,1)S(1)} %all_to_all.23.zback_ref, f32[32,128]{1,0:T(8,128)S(1)} %get-tuple-element.6.chan_ref, bf16[96,32]{1,0:T(8,128)(2,1)S(1)} %copy-done.4, ...), custom_call_target="tpu_custom_call" | custom-call | tf_op jit(solution)/shard_map/synthesize/pallas_call | solution.py:194
Async XLA Ops:
  0.6 22.7 %copy-start.3 = (bf16[64,512]{1,0:T(8,128)(2,1)S(1)}, bf16[64,512]{1,0:T(8,128)(2,1)}, u32[]{:S(2)}) copy-start(bf16[64,512]{1,0:T(8,128)(2,1)} %constant.14.clone.z_ref) | copy-start | bytes 196612
  0.6 34.4 %copy-start = (bf16[1,1,8,2,128,128]{5,4,3,2,1,0:T(8,128)(2,1)S(1)}, bf16[1,1,8,2,128,128]{5,4,3,2,1,0:T(8,128)(2,1)}, u32[]{:S(2)}) copy-start(bf16[1,1,8,2,128,128]{5,4,3,2,1,0:T(8,128)(2,1)} %w_ref.1) | copy-start | bytes 1572868
  3.2 42.3 %copy-start.2 = (bf16[512,64]{1,0:T(8,128)(2,1)S(1)}, bf16[512,64]{1,0:T(8,128)(2,1)}, u32[]{:S(2)}) copy-start(bf16[512,64]{1,0:T(8,128)(2,1)} %constant.15.clone.z_ref) | copy-start | bytes 196612
  3.2 55.9 %copy-start.1 = (bf16[2,128,192]{2,1,0:T(8,128)(2,1)S(1)}, bf16[2,128,192]{2,1,0:T(8,128)(2,1)}, u32[]{:S(2)}) copy-start(bf16[2,128,192]{2,1,0:T(8,128)(2,1)} %constant.17.clone.y_ref) | copy-start | bytes 294916
  3.3 55.9 %copy-start.4 = (bf16[96,32]{1,0:T(8,128)(2,1)S(1)}, bf16[96,32]{1,0:T(8,128)(2,1)}, u32[]{:S(2)}) copy-start(bf16[96,32]{1,0:T(8,128)(2,1)} %constant.16.clone.x_ref) | copy-start | bytes 18436

commit v7 on v6

--- a/solution.py
+++ b/solution.py
@@ -23,6 +23,8 @@
 QS = MY // PAIR
 ROWS = 16
 USED = CHANS // 2 * CELLS
+STEP = 4
+PARTS = USED // STEP
 LANES = 128
 HALF = LANES // 2
 MODES = PAIR * 2 * MZ
@@ -80,14 +82,14 @@
 
 def z_table(order):
     cosines, sines = (v.reshape(MZ, N_SPACE, CELLS) for v in phases(np.arange(MZ), NZ))
-    table = np.zeros((2, PAIR, 2, MZ, PAIR, N_SPACE, ROWS), np.float32)
+    table = np.zeros((2, PAIR, 2, MZ, PAIR, N_SPACE, USED), np.float32)
     for pair in range(PAIR):
         for cl in range(2):
             cells = slice(cl * CELLS, (cl + 1) * CELLS)
             table[0, pair, cl, :, pair, :, cells] = cosines
             table[1, pair, cl, :, pair, :, cells] = sines
-    table = table.reshape(2 * MODES, PAIR * N_SPACE, ROWS)[:, [pair * N_SPACE + space for pair, space in order]]
-    return table.reshape(2 * MODES, PAIR * N_SPACE * ROWS)
+    table = table.reshape(2 * MODES, PAIR * N_SPACE, USED)[:, [pair * N_SPACE + space for pair, space in order]]
+    return table.reshape(2 * MODES, PAIR * N_SPACE * USED)
 
 
 def x_synthesis():
@@ -146,9 +148,6 @@
     copies.append(pltpu.make_async_copy(y_hbm, y_ref, sems.at[0]))
     for copy in copies:
         copy.start()
-    for ch in range(2):
-        start = (ch * ROWS + USED) * MX
-        planes[start : start + (ROWS - USED) * MX, :] = jnp.zeros(((ROWS - USED) * MX, LANES), F32)
     copies[0].wait()
     for c in range(CHANS):
         copies[1 + 2 * c].wait()
@@ -167,10 +166,11 @@
         start = ch * ROWS * MX
         planes[start : start + USED * MX, :] = total[ch * USED * MX : (ch + 1) * USED * MX]
     for p in range(MX):
-        first = planes[pl.ds(p, ROWS, stride=MX), :]
-        second = planes[pl.ds(ROWS * MX + p, ROWS, stride=MX), :]
-        out_ref[FIRST.index((0, p))] = low_halves(first, second).astype(BF16)
-        out_ref[FIRST.index((1, p))] = high_halves(first, second).astype(BF16)
+        for part in range(PARTS):
+            first = planes[pl.ds(part * STEP * MX + p, STEP, stride=MX), :]
+            second = planes[pl.ds((ROWS + part * STEP) * MX + p, STEP, stride=MX), :]
+            out_ref[FIRST.index((0, p)), part] = low_halves(first, second).astype(BF16)
+            out_ref[FIRST.index((1, p)), part] = high_halves(first, second).astype(BF16)
 
 
 def in_hbm(values):
@@ -178,7 +178,7 @@
 
 
 def message():
-    return jax.ShapeDtypeStruct((PAIR * N_SPACE, ROWS, LANES), BF16)
+    return jax.ShapeDtypeStruct((PAIR * N_SPACE, PARTS, STEP, LANES), BF16)
 
 
 def small_message():
@@ -242,9 +242,12 @@
     return lane // HALF * 2 + lane % 2
 
 
-def sum_z_kernel(planes_ref, z_ref, out_ref):
-    planes = planes_ref[...].reshape(PAIR * N_SPACE * ROWS, LANES)
-    sums = dot(z_ref[...], planes)
+def sum_z_kernel(planes_ref, z_ref, out_ref, planes):
+    for place in range(PAIR * N_SPACE):
+        for part in range(PARTS):
+            start = place * USED + part * STEP
+            planes[start : start + STEP, :] = planes_ref[place, part].astype(F32)
+    sums = dot(z_ref[...], planes[...].astype(BF16))
     spec = sums[:MODES] + times_minus_i(sums[MODES:])
     field = index(spec.shape, 1) // (2 * QS) % 2
     zero = index(spec.shape, 0) % MZ == 0
@@ -299,8 +302,11 @@
     stacked = jnp.concatenate([spec, times_i(spec)], 0).astype(BF16)
     lane = index((1, LANES), 1) // (2 * QS) % 2
     scale = jnp.where(lane == 0, SYNTH, FORWARD).astype(F32)
-    zback = (dot(z_ref[...], stacked) * scale).astype(BF16)
-    out_ref[...] = zback.reshape(PAIR * N_SPACE, ROWS, LANES)
+    zback = dot(z_ref[...], stacked) * scale
+    for place in range(PAIR * N_SPACE):
+        for part in range(PARTS):
+            start = place * USED + part * STEP
+            out_ref[place, part] = zback[start : start + STEP].astype(BF16)
 
 
 def synthesize_kernel(
@@ -315,7 +321,8 @@
 
     for place, (pair, space) in enumerate(LAST):
         start = (pair * N_SPACE + space) * ROWS
-        planes[start : start + ROWS, :] = zback_ref[place].astype(F32)
+        for part in range(PARTS):
+            planes[start + part * STEP : start + (part + 1) * STEP, :] = zback_ref[place, part].astype(F32)
     columns = chan_ref[2 * MZ :, :].T.astype(BF16)
     fr, fi = chan_ref[:MZ, :], chan_ref[MZ : 2 * MZ, :]
     pairs = jnp.concatenate([jnp.concatenate([fr, -fi], 1), jnp.concatenate([fi, fr], 1)], 0)
@@ -393,7 +400,7 @@
 
 
 def sum_z(planes):
-    return call(sum_z_kernel, "sum_z", small_message(), planes, bf16(z_table(FIRST)))
+    return call(sum_z_kernel, "sum_z", small_message(), planes, bf16(z_table(FIRST)), scratch=[pltpu.VMEM((PAIR * N_SPACE * USED, LANES), F32)])
 
 
 def mix(spec, weights):

time: 61.6 us -> 60.5 us (0.982)
  blocking collectives: 54.4 us -> 53.3 us
    all_to_all x2, blocking collectives: 33.2 us -> 32 us  [outer(): lax.all_to_all(values, ('blk', 'space'), 0, 0, tiled=True, axis_index_gro...]
where the time goes in v7:
time: 60.5 us; the launch traced here: 60.2 us
  blocking collectives  53.3 us (88%)
  Pallas kernels  6.18 us (10%)
  between operations  0.69 us (1%)
    all_to_all x2, blocking collectives, outer(): lax.all_to_all(values, ('blk', 'space'), 0, 0, tiled=True, axis_index_gro...  32 us
    all_to_all x2, blocking collectives, inner(): lax.all_to_all(values, 'blk', 0, 0, tiled=True, axis_index_groups=groups)  21.3 us
    pallas_call x5, Pallas kernels, call(): pl.pallas_call(kernel, in_specs=in_specs or [whole] * len(operands), out_...  6.18 us

profile of v7, /device:TPU:1, one launch (start us, length us, event | category | flops | bytes accessed | tf_op | source)
XLA Modules:
  0.0 60.2 jit_solution(16423659234209607758)
XLA Ops:
  0.6 0.0 copy-start.3
  0.6 0.0 copy-start.2
  0.7 0.0 copy-start
  0.7 2.6 %analyse.1 = bf16[32,3,4,128]{3,2,1,0:T(4,128)(2,1)S(1)} custom-call(bf16[4,6,96,192]{3,2,1,0:T(8,128)(2,1)} %f_hbm.1, bf16[4,6,96,192]{3,2,1,0:T(8,128)(2,1)} %g_hbm.1, bf16[2,192,128]{2,1,0:T(8,128)(2,1)} %constant.12.clone.y_hbm, bf16[32,96]{1,0:T(8,128)(2,1)} %constant.13.clone.x_hbm), custom_call_target="tpu_custom_call" | custom-call | tf_op jit(solution)/shard_map/analyse/pallas_call | solution.py:194
  3.2 0.0 copy-start.1
  3.3 0.0 copy-start.4
  3.3 19.6 %all_to_all.20.planes_ref = bf16[32,3,4,128]{3,2,1,0:T(4,128)(2,1)S(1)} all-to-all(bf16[32,3,4,128]{3,2,1,0:T(4,128)(2,1)S(1)} %analyse.1), channel_id=1, replica_groups={{266,11,267,8,264,9,265,10,270,15,271,12,268,13,269,14,258,3,259,0,256,..., dimensions={0} | all-to-all | bytes 196608 | tf_op jit(solution)/shard_map/all_to_all | solution.py:391
  22.9 0.0 copy-done.3
  22.9 0.4 sum_z.1
  23.2 11.4 %all_to_all.21 = f32[16,2,128]{2,1,0:T(2,128)S(1)} all-to-all(f32[16,2,128]{2,1,0:T(2,128)S(1)} %bitcast.5), channel_id=1, replica_groups={{144,160,176,192,208,224,240,0,16,32,48,64,80,96,112,128},{400,416,432,..., dimensions={0} | all-to-all | bytes 32768 | tf_op jit(solution)/shard_map/all_to_all | solution.py:398
  34.7 0.0 copy-done
  34.7 0.6 %mix.1 = (f32[32,128]{1,0:T(8,128)S(1)}, f32[32,128]{1,0:T(8,128)S(1)}) custom-call(f32[32,128]{1,0:T(8,128)S(1)} %bitcast.4, bf16[1,1,8,2,128,128]{5,4,3,2,1,0:T(8,128)(2,1)S(1)} %copy-done), custom_call_target="tpu_custom_call" | custom-call | tf_op jit(solution)/shard_map/mix/pallas_call | solution.py:194
  35.3 9.9 %all_to_all.22 = f32[16,2,128]{2,1,0:T(2,128)S(1)} all-to-all(f32[16,2,128]{2,1,0:T(2,128)S(1)} %bitcast.7), channel_id=1, replica_groups={{144,160,176,192,208,224,240,0,16,32,48,64,80,96,112,128},{400,416,432,..., dimensions={0} | all-to-all | bytes 32768 | tf_op jit(solution)/shard_map/all_to_all | solution.py:398
  45.2 0.0 copy-done.2
  45.2 0.4 spread_z.1
  45.6 12.4 %all_to_all.23.zback_ref = bf16[32,3,4,128]{3,2,1,0:T(4,128)(2,1)S(1)} all-to-all(bf16[32,3,4,128]{3,2,1,0:T(4,128)(2,1)S(1)} %spread_z.1), channel_id=1, replica_groups={{266,11,267,8,264,9,265,10,270,15,271,12,268,13,269,14,258,3,259,0,256,..., dimensions={0} | all-to-all | bytes 196608 | tf_op jit(solution)/shard_map/all_to_all | solution.py:391
  58.0 0.0 copy-done.1
  58.0 0.0 copy-done.4
  58.0 2.2 %synthesize.1 = (bf16[4,6,96,192]{3,2,1,0:T(8,128)(2,1)}, bf16[4,6,96,192]{3,2,1,0:T(8,128)(2,1)}, f32[1,1,8,2,128,128]{5,4,3,2,1,0:T(8,128)}) custom-call(bf16[32,3,4,128]{3,2,1,0:T(4,128)(2,1)S(1)} %all_to_all.23.zback_ref, f32[32,128]{1,0:T(8,128)S(1)} %get-tuple-element.6.chan_ref, bf16[96,32]{1,0:T(8,128)(2,1)S(1)} %copy-done.4, ...), custom_call_target="tpu_custom_call" | custom-call | tf_op jit(solution)/shard_map/synthesize/pallas_call | solution.py:194
Async XLA Ops:
  0.6 22.3 %copy-start.3 = (bf16[64,384]{1,0:T(8,128)(2,1)S(1)}, bf16[64,384]{1,0:T(8,128)(2,1)}, u32[]{:S(2)}) copy-start(bf16[64,384]{1,0:T(8,128)(2,1)} %constant.14.clone.z_ref) | copy-start | bytes 147460
  0.6 44.5 %copy-start.2 = (bf16[384,64]{1,0:T(8,128)(2,1)S(1)}, bf16[384,64]{1,0:T(8,128)(2,1)}, u32[]{:S(2)}) copy-start(bf16[384,64]{1,0:T(8,128)(2,1)} %constant.15.clone.z_ref) | copy-start | bytes 147460
  0.7 34.0 %copy-start = (bf16[1,1,8,2,128,128]{5,4,3,2,1,0:T(8,128)(2,1)S(1)}, bf16[1,1,8,2,128,128]{5,4,3,2,1,0:T(8,128)(2,1)}, u32[]{:S(2)}) copy-start(bf16[1,1,8,2,128,128]{5,4,3,2,1,0:T(8,128)(2,1)} %w_ref.1) | copy-start | bytes 1572868
  3.2 54.8 %copy-start.1 = (bf16[2,128,192]{2,1,0:T(8,128)(2,1)S(1)}, bf16[2,128,192]{2,1,0:T(8,128)(2,1)}, u32[]{:S(2)}) copy-start(bf16[2,128,192]{2,1,0:T(8,128)(2,1)} %constant.17.clone.y_ref) | copy-start | bytes 294916
  3.3 54.8 %copy-start.4 = (bf16[96,32]{1,0:T(8,128)(2,1)S(1)}, bf16[96,32]{1,0:T(8,128)(2,1)}, u32[]{:S(2)}) copy-start(bf16[96,32]{1,0:T(8,128)(2,1)} %constant.16.clone.x_ref) | copy-start | bytes 18436

commit v8 on v7

--- a/solution.py
+++ b/solution.py
@@ -182,7 +182,22 @@
 
 
 def small_message():
-    return jax.ShapeDtypeStruct((2 * N_LINE, LANES), F32)
+    return jax.ShapeDtypeStruct((N_LINE, 2, LANES), BF16)
+
+
+def line_rows():
+    return pltpu.VMEM((2 * N_LINE, LANES), F32)
+
+
+def put_lines(out_ref, values):
+    for place in range(N_LINE):
+        out_ref[place] = values[2 * place : 2 * place + 2].astype(BF16)
+
+
+def take_lines(in_ref, rows):
+    for place in range(N_LINE):
+        rows[2 * place : 2 * place + 2, :] = in_ref[place].astype(F32)
+    return rows[...].astype(BF16)
 
 
 def field_buffer():
@@ -257,11 +272,11 @@
     spread = jnp.where(index(shape, 2) // QS == index(shape, 0), spec[None], 0.0).astype(BF16)
     spread = spread.reshape(8 * MODES, LANES)
     first, second = spread[:LANES], spread[LANES:]
-    out_ref[...] = dot_last(mode_picker(0, THERE_LINE), first) + dot_last(mode_picker(1, THERE_LINE), second)
-
-
-def mix_kernel(spec_ref, w_ref, back_ref, chan_ref):
-    wide = dot_first(spec_ref[...].astype(BF16), channel_picker(THERE_LINE)).reshape(4, 4, MZ, LANES)
+    put_lines(out_ref, dot_last(mode_picker(0, THERE_LINE), first) + dot_last(mode_picker(1, THERE_LINE), second))
+
+
+def mix_kernel(spec_ref, w_ref, back_ref, chan_ref, rows):
+    wide = dot_first(take_lines(spec_ref, rows), channel_picker(THERE_LINE)).reshape(4, 4, MZ, LANES)
     part = channel_part((4, MZ, LANES))
     spec = wide[:, 0]
     for j in range(1, 4):
@@ -285,11 +300,11 @@
     back = back.reshape(4, 1, MZ, LANES)
     shape = (4, 4, MZ, LANES)
     spread = jnp.where(channel_part(shape) == index(shape, 1), back, 0.0).astype(BF16)
-    back_ref[...] = dot_last(channel_picker(BACK_LINE), spread.reshape(LANES, LANES))
-
-
-def spread_z_kernel(back_ref, z_ref, out_ref):
-    back = back_ref[...].astype(BF16)
+    put_lines(back_ref, dot_last(channel_picker(BACK_LINE), spread.reshape(LANES, LANES)))
+
+
+def spread_z_kernel(back_ref, z_ref, out_ref, rows):
+    back = take_lines(back_ref, rows)
     owner = index((MODES, LANES), 1) // QS
     spec = jnp.zeros((MODES, LANES), F32)
     for ch in range(2):
@@ -394,9 +409,7 @@
 def inner(values, lead):
     lines = [(lead + place) % N_LINE for place in range(N_LINE)]
     groups = [[pair * N_LINE + line for line in lines] for pair in range(PAIR)]
-    values = values.reshape(N_LINE, 2, LANES)
-    values = lax.all_to_all(values, "blk", 0, 0, tiled=True, axis_index_groups=groups)
-    return values.reshape(2 * N_LINE, LANES)
+    return lax.all_to_all(values, "blk", 0, 0, tiled=True, axis_index_groups=groups)
 
 
 def sum_z(planes):
@@ -404,11 +417,12 @@
 
 
 def mix(spec, weights):
-    return call(mix_kernel, "mix", (small_message(), small_message()), spec, weights)
+    channels = jax.ShapeDtypeStruct((4 * MZ, LANES), F32)
+    return call(mix_kernel, "mix", (small_message(), channels), spec, weights, scratch=[line_rows()])
 
 
 def spread_z(back):
-    return call(spread_z_kernel, "spread_z", message(), back, bf16(z_table(LAST).T))
+    return call(spread_z_kernel, "spread_z", message(), back, bf16(z_table(LAST).T), scratch=[line_rows()])
 
 
 def shards(input_field, cotangent, weights):

time: 60.5 us -> 60.1 us (level)
  blocking collectives: 53.3 us -> 52.5 us
    all_to_all x2, blocking collectives: 21.3 us -> 20.6 us  [inner(): lax.all_to_all(values, 'blk', 0, 0, tiled=True, axis_index_groups=groups)]
where the time goes in v8:
time: 60.1 us; the launch traced here: 59.5 us
  blocking collectives  52.5 us (87%)
  Pallas kernels  6.22 us (10%)
  between operations  0.69 us (1%)
    all_to_all x2, blocking collectives, outer(): lax.all_to_all(values, ('blk', 'space'), 0, 0, tiled=True, axis_index_gro...  31.9 us
    all_to_all x2, blocking collectives, inner(): lax.all_to_all(values, 'blk', 0, 0, tiled=True, axis_index_groups=groups)  20.6 us
    pallas_call x5, Pallas kernels, call(): pl.pallas_call(kernel, in_specs=in_specs or [whole] * len(operands), out_...  6.22 us

profile of v8, /device:TPU:1, one launch (start us, length us, event | category | flops | bytes accessed | tf_op | source)
XLA Modules:
  0.0 59.5 jit_solution(9791572751623024045)
XLA Ops:
  0.6 0.0 copy-start.3
  0.6 0.0 copy-start.2
  0.7 0.0 copy-start
  0.7 2.6 %analyse.1 = bf16[32,3,4,128]{3,2,1,0:T(4,128)(2,1)S(1)} custom-call(bf16[4,6,96,192]{3,2,1,0:T(8,128)(2,1)} %f_hbm.1, bf16[4,6,96,192]{3,2,1,0:T(8,128)(2,1)} %g_hbm.1, bf16[2,192,128]{2,1,0:T(8,128)(2,1)} %constant.12.clone.y_hbm, bf16[32,96]{1,0:T(8,128)(2,1)} %constant.13.clone.x_hbm), custom_call_target="tpu_custom_call" | custom-call | tf_op jit(solution)/shard_map/analyse/pallas_call | solution.py:209
  3.2 0.0 copy-start.1
  3.3 0.0 copy-start.4
  3.3 19.6 %all_to_all.20.planes_ref = bf16[32,3,4,128]{3,2,1,0:T(4,128)(2,1)S(1)} all-to-all(bf16[32,3,4,128]{3,2,1,0:T(4,128)(2,1)S(1)} %analyse.1), channel_id=1, replica_groups={{266,11,267,8,264,9,265,10,270,15,271,12,268,13,269,14,258,3,259,0,256,..., dimensions={0} | all-to-all | bytes 196608 | tf_op jit(solution)/shard_map/all_to_all | solution.py:406
  22.9 0.0 copy-done.3
  22.9 0.4 sum_z.1
  23.2 11.2 %all_to_all.21.spec_ref = bf16[16,2,128]{2,1,0:T(2,128)(2,1)S(1)} all-to-all(bf16[16,2,128]{2,1,0:T(2,128)(2,1)S(1)} %sum_z.1), channel_id=1, replica_groups={{144,160,176,192,208,224,240,0,16,32,48,64,80,96,112,128},{400,416,432,..., dimensions={0} | all-to-all | bytes 16384 | tf_op jit(solution)/shard_map/all_to_all | solution.py:412
  34.4 0.0 copy-done
  34.4 0.7 %mix.1 = (bf16[16,2,128]{2,1,0:T(2,128)(2,1)S(1)}, f32[32,128]{1,0:T(8,128)S(1)}) custom-call(bf16[16,2,128]{2,1,0:T(2,128)(2,1)S(1)} %all_to_all.21.spec_ref, bf16[1,1,8,2,128,128]{5,4,3,2,1,0:T(8,128)(2,1)S(1)} %copy-done), custom_call_target="tpu_custom_call" | custom-call | tf_op jit(solution)/shard_map/mix/pallas_call | solution.py:209
  35.1 9.5 %all_to_all.22.back_ref = bf16[16,2,128]{2,1,0:T(2,128)(2,1)S(1)} all-to-all(bf16[16,2,128]{2,1,0:T(2,128)(2,1)S(1)} %get-tuple-element.5), channel_id=1, replica_groups={{144,160,176,192,208,224,240,0,16,32,48,64,80,96,112,128},{400,416,432,..., dimensions={0} | all-to-all | bytes 16384 | tf_op jit(solution)/shard_map/all_to_all | solution.py:412
  44.5 0.0 copy-done.2
  44.5 0.4 spread_z.1
  45.0 12.3 %all_to_all.23.zback_ref = bf16[32,3,4,128]{3,2,1,0:T(4,128)(2,1)S(1)} all-to-all(bf16[32,3,4,128]{3,2,1,0:T(4,128)(2,1)S(1)} %spread_z.1), channel_id=1, replica_groups={{266,11,267,8,264,9,265,10,270,15,271,12,268,13,269,14,258,3,259,0,256,..., dimensions={0} | all-to-all | bytes 196608 | tf_op jit(solution)/shard_map/all_to_all | solution.py:406
  57.3 0.0 copy-done.1
  57.3 0.0 copy-done.4
  57.3 2.2 %synthesize.1 = (bf16[4,6,96,192]{3,2,1,0:T(8,128)(2,1)}, bf16[4,6,96,192]{3,2,1,0:T(8,128)(2,1)}, f32[1,1,8,2,128,128]{5,4,3,2,1,0:T(8,128)}) custom-call(bf16[32,3,4,128]{3,2,1,0:T(4,128)(2,1)S(1)} %all_to_all.23.zback_ref, f32[32,128]{1,0:T(8,128)S(1)} %get-tuple-element.6.chan_ref, bf16[96,32]{1,0:T(8,128)(2,1)S(1)} %copy-done.4, ...), custom_call_target="tpu_custom_call" | custom-call | tf_op jit(solution)/shard_map/synthesize/pallas_call | solution.py:209
Async XLA Ops:
  0.6 22.3 %copy-start.3 = (bf16[64,384]{1,0:T(8,128)(2,1)S(1)}, bf16[64,384]{1,0:T(8,128)(2,1)}, u32[]{:S(2)}) copy-start(bf16[64,384]{1,0:T(8,128)(2,1)} %constant.14.clone.z_ref) | copy-start | bytes 147460
  0.6 43.9 %copy-start.2 = (bf16[384,64]{1,0:T(8,128)(2,1)S(1)}, bf16[384,64]{1,0:T(8,128)(2,1)}, u32[]{:S(2)}) copy-start(bf16[384,64]{1,0:T(8,128)(2,1)} %constant.15.clone.z_ref) | copy-start | bytes 147460
  0.7 33.7 %copy-start = (bf16[1,1,8,2,128,128]{5,4,3,2,1,0:T(8,128)(2,1)S(1)}, bf16[1,1,8,2,128,128]{5,4,3,2,1,0:T(8,128)(2,1)}, u32[]{:S(2)}) copy-start(bf16[1,1,8,2,128,128]{5,4,3,2,1,0:T(8,128)(2,1)} %w_ref.1) | copy-start | bytes 1572868
  3.2 54.0 %copy-start.1 = (bf16[2,128,192]{2,1,0:T(8,128)(2,1)S(1)}, bf16[2,128,192]{2,1,0:T(8,128)(2,1)}, u32[]{:S(2)}) copy-start(bf16[2,128,192]{2,1,0:T(8,128)(2,1)} %constant.17.clone.y_ref) | copy-start | bytes 294916
  3.3 54.0 %copy-start.4 = (bf16[96,32]{1,0:T(8,128)(2,1)S(1)}, bf16[96,32]{1,0:T(8,128)(2,1)}, u32[]{:S(2)}) copy-start(bf16[96,32]{1,0:T(8,128)(2,1)} %constant.16.clone.x_ref) | copy-start | bytes 18436

commit v9 on v8

--- a/solution.py
+++ b/solution.py
@@ -166,11 +166,11 @@
         start = ch * ROWS * MX
         planes[start : start + USED * MX, :] = total[ch * USED * MX : (ch + 1) * USED * MX]
     for p in range(MX):
-        for part in range(PARTS):
-            first = planes[pl.ds(part * STEP * MX + p, STEP, stride=MX), :]
-            second = planes[pl.ds((ROWS + part * STEP) * MX + p, STEP, stride=MX), :]
-            out_ref[FIRST.index((0, p)), part] = low_halves(first, second).astype(BF16)
-            out_ref[FIRST.index((1, p)), part] = high_halves(first, second).astype(BF16)
+        first = planes[pl.ds(p, USED, stride=MX), :]
+        second = planes[pl.ds(ROWS * MX + p, USED, stride=MX), :]
+        for pair, chosen in enumerate((low_halves(first, second), high_halves(first, second))):
+            for part in range(PARTS):
+                out_ref[FIRST.index((pair, p)), part] = chosen[part * STEP : (part + 1) * STEP].astype(BF16)
 
 
 def in_hbm(values):

time: 60.1 us -> 60.1 us (level)
  no operation moved by 1% of the time
where the time goes in v9:
time: 60.1 us; the launch traced here: 59.5 us
  blocking collectives  52.5 us (87%)
  Pallas kernels  6.21 us (10%)
  between operations  0.69 us (1%)
    all_to_all x2, blocking collectives, outer(): lax.all_to_all(values, ('blk', 'space'), 0, 0, tiled=True, axis_index_gro...  31.9 us
    all_to_all x2, blocking collectives, inner(): lax.all_to_all(values, 'blk', 0, 0, tiled=True, axis_index_groups=groups)  20.6 us
    pallas_call x5, Pallas kernels, call(): pl.pallas_call(kernel, in_specs=in_specs or [whole] * len(operands), out_...  6.21 us

profile of v9, /device:TPU:1, one launch (start us, length us, event | category | flops | bytes accessed | tf_op | source)
XLA Modules:
  0.0 59.5 jit_solution(2743388644418470110)
XLA Ops:
  0.6 0.0 copy-start.3
  0.6 0.0 copy-start.2
  0.7 0.0 copy-start
  0.7 2.6 %analyse.1 = bf16[32,3,4,128]{3,2,1,0:T(4,128)(2,1)S(1)} custom-call(bf16[4,6,96,192]{3,2,1,0:T(8,128)(2,1)} %f_hbm.1, bf16[4,6,96,192]{3,2,1,0:T(8,128)(2,1)} %g_hbm.1, bf16[2,192,128]{2,1,0:T(8,128)(2,1)} %constant.12.clone.y_hbm, bf16[32,96]{1,0:T(8,128)(2,1)} %constant.13.clone.x_hbm), custom_call_target="tpu_custom_call" | custom-call | tf_op jit(solution)/shard_map/analyse/pallas_call | solution.py:209
  3.2 0.0 copy-start.1
  3.3 0.0 copy-start.4
  3.3 19.6 %all_to_all.20.planes_ref = bf16[32,3,4,128]{3,2,1,0:T(4,128)(2,1)S(1)} all-to-all(bf16[32,3,4,128]{3,2,1,0:T(4,128)(2,1)S(1)} %analyse.1), channel_id=1, replica_groups={{266,11,267,8,264,9,265,10,270,15,271,12,268,13,269,14,258,3,259,0,256,..., dimensions={0} | all-to-all | bytes 196608 | tf_op jit(solution)/shard_map/all_to_all | solution.py:406
  22.9 0.0 copy-done.3
  22.9 0.4 sum_z.1
  23.2 11.2 %all_to_all.21.spec_ref = bf16[16,2,128]{2,1,0:T(2,128)(2,1)S(1)} all-to-all(bf16[16,2,128]{2,1,0:T(2,128)(2,1)S(1)} %sum_z.1), channel_id=1, replica_groups={{144,160,176,192,208,224,240,0,16,32,48,64,80,96,112,128},{400,416,432,..., dimensions={0} | all-to-all | bytes 16384 | tf_op jit(solution)/shard_map/all_to_all | solution.py:412
  34.4 0.0 copy-done
  34.4 0.7 %mix.1 = (bf16[16,2,128]{2,1,0:T(2,128)(2,1)S(1)}, f32[32,128]{1,0:T(8,128)S(1)}) custom-call(bf16[16,2,128]{2,1,0:T(2,128)(2,1)S(1)} %all_to_all.21.spec_ref, bf16[1,1,8,2,128,128]{5,4,3,2,1,0:T(8,128)(2,1)S(1)} %copy-done), custom_call_target="tpu_custom_call" | custom-call | tf_op jit(solution)/shard_map/mix/pallas_call | solution.py:209
  35.0 9.5 %all_to_all.22.back_ref = bf16[16,2,128]{2,1,0:T(2,128)(2,1)S(1)} all-to-all(bf16[16,2,128]{2,1,0:T(2,128)(2,1)S(1)} %get-tuple-element.5), channel_id=1, replica_groups={{144,160,176,192,208,224,240,0,16,32,48,64,80,96,112,128},{400,416,432,..., dimensions={0} | all-to-all | bytes 16384 | tf_op jit(solution)/shard_map/all_to_all | solution.py:412
  44.5 0.0 copy-done.2
  44.5 0.4 spread_z.1
  45.0 12.3 %all_to_all.23.zback_ref = bf16[32,3,4,128]{3,2,1,0:T(4,128)(2,1)S(1)} all-to-all(bf16[32,3,4,128]{3,2,1,0:T(4,128)(2,1)S(1)} %spread_z.1), channel_id=1, replica_groups={{266,11,267,8,264,9,265,10,270,15,271,12,268,13,269,14,258,3,259,0,256,..., dimensions={0} | all-to-all | bytes 196608 | tf_op jit(solution)/shard_map/all_to_all | solution.py:406
  57.3 0.0 copy-done.1
  57.3 0.0 copy-done.4
  57.3 2.2 %synthesize.1 = (bf16[4,6,96,192]{3,2,1,0:T(8,128)(2,1)}, bf16[4,6,96,192]{3,2,1,0:T(8,128)(2,1)}, f32[1,1,8,2,128,128]{5,4,3,2,1,0:T(8,128)}) custom-call(bf16[32,3,4,128]{3,2,1,0:T(4,128)(2,1)S(1)} %all_to_all.23.zback_ref, f32[32,128]{1,0:T(8,128)S(1)} %get-tuple-element.6.chan_ref, bf16[96,32]{1,0:T(8,128)(2,1)S(1)} %copy-done.4, ...), custom_call_target="tpu_custom_call" | custom-call | tf_op jit(solution)/shard_map/synthesize/pallas_call | solution.py:209
Async XLA Ops:
  0.6 22.2 %copy-start.3 = (bf16[64,384]{1,0:T(8,128)(2,1)S(1)}, bf16[64,384]{1,0:T(8,128)(2,1)}, u32[]{:S(2)}) copy-start(bf16[64,384]{1,0:T(8,128)(2,1)} %constant.14.clone.z_ref) | copy-start | bytes 147460
  0.6 43.9 %copy-start.2 = (bf16[384,64]{1,0:T(8,128)(2,1)S(1)}, bf16[384,64]{1,0:T(8,128)(2,1)}, u32[]{:S(2)}) copy-start(bf16[384,64]{1,0:T(8,128)(2,1)} %constant.15.clone.z_ref) | copy-start | bytes 147460
  0.7 33.7 %copy-start = (bf16[1,1,8,2,128,128]{5,4,3,2,1,0:T(8,128)(2,1)S(1)}, bf16[1,1,8,2,128,128]{5,4,3,2,1,0:T(8,128)(2,1)}, u32[]{:S(2)}) copy-start(bf16[1,1,8,2,128,128]{5,4,3,2,1,0:T(8,128)(2,1)} %w_ref.1) | copy-start | bytes 1572868
  3.2 54.0 %copy-start.1 = (bf16[2,128,192]{2,1,0:T(8,128)(2,1)S(1)}, bf16[2,128,192]{2,1,0:T(8,128)(2,1)}, u32[]{:S(2)}) copy-start(bf16[2,128,192]{2,1,0:T(8,128)(2,1)} %constant.17.clone.y_ref) | copy-start | bytes 294916
  3.3 54.0 %copy-start.4 = (bf16[96,32]{1,0:T(8,128)(2,1)S(1)}, bf16[96,32]{1,0:T(8,128)(2,1)}, u32[]{:S(2)}) copy-start(bf16[96,32]{1,0:T(8,128)(2,1)} %constant.16.clone.x_ref) | copy-start | bytes 18436
